TPU v7x, 32 devices: a whole 2x2x4 slice. The times are simulated.
32 devices in a mesh: exp: 4 (over y, x), fsdp: 8 (over z, core).
Axes of the slice: x: 2, y: 2, z: 4, core: 2. Of those that a mesh axis runs over, the one named last changes fastest.
Arguments:
- tokens: bfloat16 [1024, 3072], P('fsdp'), may hold values from -6 to 6
- out_grad: bfloat16 [1024, 3072], P('fsdp'), may hold values from -6 to 6
- experts_chosen: int32 [1024, 2], P('fsdp'), may hold values from 0 to 3, all different within a row; in each aligned block of 128 rows (0 to 127, 128 to 255, ...) at most 80 rows name the same one
- route_weight: float32 [1024, 2], P('fsdp'), may hold values from 0.1 to 0.9
- w_gate: bfloat16 [4, 3072, 8192], P('exp', None, 'fsdp'), may hold values from -0.109375 to 0.109375
- w_up: bfloat16 [4, 3072, 8192], P('exp', None, 'fsdp'), may hold values from -0.109375 to 0.109375
- w_down: bfloat16 [4, 8192, 3072], P('exp', 'fsdp'), may hold values from -0.0625 to 0.0625
- projection: bfloat16 [512, 3072], P(None, 'fsdp'), may hold values from -0.109375 to 0.109375
- mom_gate: float32 [4, 512, 8192], P('exp', None, 'fsdp'), may hold values from -3 to 3
- mom_up: float32 [4, 512, 8192], P('exp', None, 'fsdp'), may hold values from -3 to 3
- mom_down: float32 [4, 8192, 512], P('exp', 'fsdp'), may hold values from -3 to 3
Outputs:
- grad_tokens: bfloat16 [1024, 3072], P('fsdp')
- new_gate_mom: float32 [4, 512, 8192], P('exp', None, 'fsdp')
- new_up_mom: float32 [4, 512, 8192], P('exp', None, 'fsdp')
- new_down_mom: float32 [4, 8192, 512], P('exp', 'fsdp')
Inputs may be any that keep to these rules, and one draw needn't show every extreme that they name: `experts_chosen`: each row names 2 different experts. In each aligned block of 128 rows no expert is named by more than 80 rows, a bound that some block reaches.
All inputs are finite; a program needn't handle non-finite values.
Results may differ from a plain program's by a relative error of at most 0.015.
Values may be sent and summed in bfloat16 or wider, within the bound.
No kernel may reach another device: no remote copies, remote signals or barrier semaphores. Data moves between devices by JAX's collectives and lax.ppermute only.
A program may use at most 128 MiB of HBM per device.

v0:
```python
import jax
import jax.numpy as jnp
from jax import lax
from jax.sharding import PartitionSpec as P

momentum_decay = 0.9
grad_share = 0.1


def contract_last(left, right):
    return lax.dot_general(
        left, right, (((1,), (1,)), ((), ())), preferred_element_type=jnp.float32
    )


def contract_first(left, right):
    return lax.dot_general(
        left, right, (((0,), (0,)), ((), ())), preferred_element_type=jnp.float32
    )


def shards(
    tokens,
    out_grad,
    experts_chosen,
    route_weight,
    w_gate,
    w_up,
    w_down,
    projection,
    mom_gate,
    mom_up,
    mom_down,
):
    tok_count = tokens.shape[0]
    top_count = experts_chosen.shape[1]
    hidden_local = w_gate.shape[2]
    experts_all = lax.axis_size("exp") * w_gate.shape[0]
    capacity = min(tok_count, tok_count * top_count * 5 // (4 * experts_all))
    expert = lax.axis_index("exp") * w_gate.shape[0]
    gate_weight = w_gate[0]
    up_weight = w_up[0]
    down_weight = w_down[0]
    hit = experts_chosen == expert
    member = jnp.any(hit, axis=1).astype(jnp.int32)
    route = jnp.sum(jnp.where(hit, route_weight, jnp.zeros_like(route_weight)), axis=1)
    slot_pos = jnp.cumsum(member, dtype=jnp.int32) - 1
    places = lax.broadcasted_iota(jnp.int32, (capacity, tok_count), 0)
    select_mat = ((slot_pos[None, :] == places) & (member[None, :] > 0)).astype(jnp.bfloat16)
    x_send = jnp.dot(select_mat, tokens, preferred_element_type=jnp.float32).astype(jnp.bfloat16)
    scaled = (route[:, None] * out_grad).astype(jnp.bfloat16)
    grad_send = jnp.dot(select_mat, scaled, preferred_element_type=jnp.float32).astype(jnp.bfloat16)
    proj_full = lax.all_gather(projection, "fsdp", axis=1, tiled=True)
    lowrank_tok = contract_last(x_send, proj_full).astype(jnp.bfloat16)
    lowrank_grad = contract_last(grad_send, proj_full).astype(jnp.bfloat16)
    low_tokens, low_grad = (
        lax.all_gather(lowrank_tok, "fsdp", axis=0, tiled=True),
        lax.all_gather(lowrank_grad, "fsdp", axis=0, tiled=True),
    )
    fwd_matrix = jnp.concatenate([gate_weight, up_weight], axis=1)
    x_all, grad_all = (
        lax.all_gather(x_send, "fsdp", axis=0, tiled=True),
        lax.all_gather(grad_send, "fsdp", axis=0, tiled=True),
    )
    fwd_out = jnp.dot(x_all, fwd_matrix, preferred_element_type=jnp.float32)
    gate = fwd_out[:, :hidden_local]
    up = fwd_out[:, hidden_local : 2 * hidden_local]
    sigma = jax.nn.sigmoid(gate)
    silu = gate * sigma
    hidden = (silu * up).astype(jnp.bfloat16)
    bwd_out = contract_last(grad_all, down_weight)
    d_gate = (bwd_out * up * sigma * (1.0 + gate * (1.0 - sigma))).astype(jnp.bfloat16)
    d_up = (bwd_out * silu).astype(jnp.bfloat16)
    my_rows = lax.psum_scatter(
        (contract_last(d_gate, gate_weight) + contract_last(d_up, up_weight)).astype(jnp.bfloat16),
        "fsdp",
        scatter_dimension=0,
        tiled=True,
    ).astype(jnp.float32)
    tok_grad = lax.dot_general(
        select_mat.astype(jnp.float32),
        my_rows,
        (((0,), (0,)), ((), ())),
        precision=lax.Precision.HIGHEST,
        preferred_element_type=jnp.float32,
    )
    grad_tokens = lax.psum(tok_grad.astype(jnp.bfloat16), "exp")
    new_gate = momentum_decay * mom_gate + grad_share * contract_first(low_tokens, d_gate)[None]
    new_up = momentum_decay * mom_up + grad_share * contract_first(low_tokens, d_up)[None]
    new_down = momentum_decay * mom_down + grad_share * contract_first(hidden, low_grad)[None]
    return (grad_tokens, new_gate, new_up, new_down)


def solution(mesh):
    in_specs = (
        P("fsdp", None),
        P("fsdp", None),
        P("fsdp", None),
        P("fsdp", None),
        P("exp", None, "fsdp"),
        P("exp", None, "fsdp"),
        P("exp", "fsdp", None),
        P(None, "fsdp"),
        P("exp", None, "fsdp"),
        P("exp", None, "fsdp"),
        P("exp", "fsdp", None),
    )
    out_specs = (
        P("fsdp", None),
        P("exp", None, "fsdp"),
        P("exp", None, "fsdp"),
        P("exp", "fsdp", None),
    )
    return jax.shard_map(shards, mesh=mesh, in_specs=in_specs, out_specs=out_specs, check_vma=False)
```

profile of v0, /device:TPU:0, one launch (start us, length us, event | category | flops | bytes accessed | tf_op | source)
XLA Modules:
  0.0 258.9 jit_solution(15281953478488487516)
XLA Ops:
  7.2 0.0 copy-start
  7.2 0.0 all-gather.6.cloned.1.call-start
  7.2 0.8 fusion.24
  8.0 0.1 copy.16
  8.1 0.2 reduce-window.8
  8.3 0.1 add_reduce_fusion
  8.4 0.0 copy-done
  8.4 1.1 convolution_convert_fusion.1
  9.5 0.0 all-gather.6.cloned.1.call-update
  9.5 0.0 all-gather.4.cloned.1.call-start
  9.6 0.7 select_reduce_fusion
  10.3 2.3 convolution_convert_fusion.2
  12.6 0.0 all-gather.4.cloned.1.call-update
  12.6 0.0 all-gather.8.cloned.1.call-start
  12.6 0.7 all-gather.8.cloned.1.call-update
  13.3 0.0 reduce-scatter.2.cloned.1.call-start
  13.4 44.4 %all-gather.6.cloned.1.call-done = bf16[640,3072]{1,0:T(8,128)(2,1)} async-done(((bf16[80,3072]{1,0:T(8,128)(2,1)}), bf16[640,3072]{1,0:T(8,128)(2,1)}) %all-gather.6.cloned.1.call-update) | async-done | bytes 3932176 | tf_op jit(solution)/shard_map/all_gather | solution.py:62
  57.7 16.3 %fusion = f32[640,2048]{1,0:T(8,128)} fusion(bf16[640,3072]{1,0:T(8,128)(2,1)} %all-gather.6.cloned.1.call-done, bf16[3072,1024]{1,0:T(8,128)(2,1)} %bitcast.35, bf16[3072,1024]{1,0:T(8,128)(2,1)} %bitcast.34), kind=kOutput, calls=%fused_computation | convolution fusion | flops 8078229504 | bytes 21757952 | tf_op jit(solution)/shard_map/dot_general | solution.py:65
  74.1 29.5 %all-gather.4.cloned.1.call-done = bf16[640,3072]{1,0:T(8,128)(2,1)} async-done(((bf16[80,3072]{1,0:T(8,128)(2,1)}), bf16[640,3072]{1,0:T(8,128)(2,1)}) %all-gather.4.cloned.1.call-update) | async-done | bytes 3932176 | tf_op jit(solution)/shard_map/all_gather | solution.py:63
  103.6 10.4 %multiply_convert_fusion.1 = (bf16[640,1024]{1,0:T(8,128)(2,1)S(1)}, bf16[640,1024]{1,0:T(8,128)(2,1)S(1)}) fusion(f32[640,2048]{1,0:T(8,128)} %fusion, bf16[640,3072]{1,0:T(8,128)(2,1)} %all-gather.4.cloned.1.call-done, bf16[1,1024,3072]{2,1,0:T(8,128)(2,1)} %param.17), kind=kOutput, calls=%fused_computation.11 | convolution fusion | flops 4035051520 | bytes 18087936 | tf_op jit(solution)/shard_map/dot_general | solution.py:11
  114.0 0.0 copy-start.7
  114.0 0.0 copy-start.8
  114.0 7.3 %fusion.21 = f32[640,3072]{1,0:T(8,128)S(1)} fusion(bf16[640,1024]{1,0:T(8,128)(2,1)S(1)} %get-tuple-element.5, bf16[1,3072,1024]{2,1,0:T(8,128)(2,1)} %param.15), kind=kOutput, calls=%fused_computation.37 | convolution fusion | flops 4026531840 | bytes 15466496 | tf_op jit(solution)/shard_map/dot_general | solution.py:11
  121.3 0.0 copy-done.7
  121.3 0.0 copy-done.8
  121.3 9.0 %add_convert_fusion = bf16[640,3072]{1,0:T(8,128)(2,1)} fusion(f32[640,3072]{1,0:T(8,128)S(1)} %fusion.21, bf16[640,1024]{1,0:T(8,128)(2,1)S(1)} %get-tuple-element.4, bf16[1,3072,1024]{2,1,0:T(8,128)(2,1)} %param.16), kind=kOutput, calls=%fused_computation.4 | convolution fusion | flops 4030464000 | bytes 19398656 | tf_op jit(solution)/shard_map/dot_general | solution.py:11
  130.3 0.0 reduce-scatter.2.cloned.1.call-update
  130.3 0.0 copy-start.4
  130.3 0.0 all-reduce.2.cloned.1.call-start
  130.4 11.9 %all-gather.8.cloned.1.call-done = bf16[512,3072]{1,0:T(8,128)(2,1)} async-done(((bf16[512,384]{1,0:T(8,128)(2,1)}), bf16[512,3072]{1,0:T(8,128)(2,1)}) %all-gather.8.cloned.1.call-update) | async-done | bytes 3145744 | tf_op jit(solution)/shard_map/all_gather | solution.py:53
  142.3 0.0 copy-done.3
  142.3 3.1 %convolution_convert_fusion.4 = bf16[80,512]{1,0:T(8,128)(2,1)S(1)} fusion(bf16[80,3072]{1,0:T(8,128)(2,1)S(1)} %copy-done.3, bf16[512,3072]{1,0:T(8,128)(2,1)} %all-gather.8.cloned.1.call-done), kind=kOutput, calls=%fused_computation.20 | convolution fusion | flops 251699200 | bytes 3719168 | tf_op jit(solution)/shard_map/dot_general | solution.py:11
  145.4 0.0 copy-start.9
  145.5 18.0 %all_gather.18 = bf16[640,512]{1,0:T(8,128)(2,1)S(1)} all-gather(bf16[80,512]{1,0:T(8,128)(2,1)S(1)} %convolution_convert_fusion.4), channel_id=1, replica_groups=mesh['exp'=4,'fsdp'=8] {'fsdp'}, dimensions={0}, use_global_device_ids=true | all-gather | bytes 737280 | tf_op jit(solution)/shard_map/all_gather | solution.py:57
  163.5 0.0 copy-done.4
  163.5 0.0 copy-done.2
  163.5 1.1 convolution_convert_fusion.3
  164.6 18.4 %all_gather.19 = bf16[640,512]{1,0:T(8,128)(2,1)S(1)} all-gather(bf16[80,512]{1,0:T(8,128)(2,1)S(1)} %convolution_convert_fusion.3), channel_id=1, replica_groups=mesh['exp'=4,'fsdp'=8] {'fsdp'}, dimensions={0}, use_global_device_ids=true | all-gather | bytes 737280 | tf_op jit(solution)/shard_map/all_gather | solution.py:58
  183.0 0.0 copy-done.5
  183.0 2.3 bitcast_add_fusion.1
  185.3 14.5 %reduce-scatter.2.cloned.1.call-done = bf16[80,3072]{1,0:T(8,128)(2,1)} async-done(((bf16[640,3072]{1,0:T(8,128)(2,1)}), bf16[80,3072]{1,0:T(8,128)(2,1)}) %reduce-scatter.2.cloned.1.call-update) | async-done | bytes 491536 | tf_op jit(solution)/shard_map/reduce_scatter | solution.py:74
  199.9 2.3 convolution_convert_fusion
  202.2 0.0 all-reduce.2.cloned.1.call-update
  202.2 0.0 copy-start.10
  202.2 3.8 %bitcast_add_fusion.2 = f32[1,512,1024]{2,1,0:T(8,128)} fusion(f32[1,512,1024]{2,1,0:T(8,128)S(1)} %copy-done.6, bf16[640,512]{1,0:T(8,128)(2,1)S(1)} %all_gather.18, bf16[640,1024]{1,0:T(8,128)(2,1)} %copy-done.7), kind=kOutput, calls=%fused_computation.17 | convolution fusion | flops 672661504 | bytes 6160384 | tf_op jit(solution)/shard_map/dot_general | solution.py:17
  206.0 5.2 %bitcast_add_fusion = f32[1,1024,512]{2,1,0:T(8,128)} fusion(f32[1,1024,512]{2,1,0:T(8,128)S(1)} %copy-done.10, bf16[640,512]{1,0:T(8,128)(2,1)S(1)} %all_gather.19, f32[640,2048]{1,0:T(8,128)} %fusion), kind=kOutput, calls=%fused_computation.15 | convolution fusion | flops 676593664 | bytes 10092544 | tf_op jit(solution)/shard_map/dot_general | solution.py:17
  211.3 39.1 %all-reduce.2.cloned.1.call-done = bf16[128,3072]{1,0:T(8,128)(2,1)} async-done(((bf16[128,3072]{1,0:T(8,128)(2,1)}), bf16[128,3072]{1,0:T(8,128)(2,1)}) %all-reduce.2.cloned.1.call-update) | async-done | bytes 786448 | tf_op jit(solution)/shard_map/psum | solution.py:87
  250.3 2.1 copy.18
  (10 shorter events, 0.0 us)
Async XLA Ops:
  7.2 1.2 copy-start
  7.2 50.6 %all-gather.6.cloned.1.call-start = ((), (), s32[]{:S(2)}) async-start(), calls=%async_computation.2 | async-start | bytes 4423680 | tf_op jit(solution)/shard_map/all_gather | solution.py:62
  9.5 94.1 %all-gather.4.cloned.1.call-start = ((), (), s32[]{:S(2)}) async-start(), calls=%async_computation.1 | async-start | bytes 4423680 | tf_op jit(solution)/shard_map/all_gather | solution.py:63
  12.6 129.7 %all-gather.8.cloned.1.call-start = ((), (), s32[]{:S(2)}) async-start(), calls=%async_computation.5 | async-start | bytes 3538944 | tf_op jit(solution)/shard_map/all_gather | solution.py:53
  13.3 186.5 %reduce-scatter.2.cloned.1.call-start = ((), (), s32[]{:S(2)}) async-start(), calls=%async_computation.3 | async-start | bytes 4423680 | tf_op jit(solution)/shard_map/reduce_scatter | solution.py:74
  114.0 7.3 %copy-start.7 = (bf16[640,1024]{1,0:T(8,128)(2,1)}, bf16[640,1024]{1,0:T(8,128)(2,1)S(1)}, u32[]{:S(2)}) copy-start(bf16[640,1024]{1,0:T(8,128)(2,1)S(1)} %get-tuple-element.5) | copy-start | bytes 3932164
  114.0 7.3 %copy-start.8 = (bf16[640,1024]{1,0:T(8,128)(2,1)}, bf16[640,1024]{1,0:T(8,128)(2,1)S(1)}, u32[]{:S(2)}) copy-start(bf16[640,1024]{1,0:T(8,128)(2,1)S(1)} %get-tuple-element.4) | copy-start | bytes 3932164
  130.3 12.0 %copy-start.3 = (bf16[80,3072]{1,0:T(8,128)(2,1)S(1)}, bf16[80,3072]{1,0:T(8,128)(2,1)}, u32[]{:S(2)}) copy-start(bf16[80,3072]{1,0:T(8,128)(2,1)} %convolution_convert_fusion.1) | copy-start | bytes 1474564
  130.3 33.2 %copy-start.4 = (bf16[80,3072]{1,0:T(8,128)(2,1)S(1)}, bf16[80,3072]{1,0:T(8,128)(2,1)}, u32[]{:S(2)}) copy-start(bf16[80,3072]{1,0:T(8,128)(2,1)} %convolution_convert_fusion.2) | copy-start | bytes 1474564
  130.3 120.0 %all-reduce.2.cloned.1.call-start = ((), (), s32[]{:S(2)}) async-start(), calls=%async_computation.4 | async-start | bytes 1572864 | tf_op jit(solution)/shard_map/psum | solution.py:87
  142.3 21.2 %copy-start.2 = (bf16[512,3072]{1,0:T(8,128)(2,1)S(1)}, bf16[512,3072]{1,0:T(8,128)(2,1)}, u32[]{:S(2)}) copy-start(bf16[512,3072]{1,0:T(8,128)(2,1)} %all-gather.8.cloned.1.call-done) | copy-start | bytes 9437188
  145.4 37.5 %copy-start.5 = (f32[1,512,1024]{2,1,0:T(8,128)S(1)}, f32[1,512,1024]{2,1,0:T(8,128)}, u32[]{:S(2)}) copy-start(f32[1,512,1024]{2,1,0:T(8,128)} %param.20) | copy-start | bytes 6291460
  145.4 37.5 %copy-start.9 = (bf16[640,1024]{1,0:T(8,128)(2,1)S(1)}, bf16[640,1024]{1,0:T(8,128)(2,1)}, u32[]{:S(2)}) copy-start(bf16[640,1024]{1,0:T(8,128)(2,1)} %copy-done.8) | copy-start | bytes 3932164
  183.0 19.2 %copy-start.6 = (f32[1,512,1024]{2,1,0:T(8,128)S(1)}, f32[1,512,1024]{2,1,0:T(8,128)}, u32[]{:S(2)}) copy-start(f32[1,512,1024]{2,1,0:T(8,128)} %param.19) | copy-start | bytes 6291460
  202.2 3.8 %copy-start.10 = (f32[1,1024,512]{2,1,0:T(8,128)S(1)}, f32[1,1024,512]{2,1,0:T(8,128)}, u32[]{:S(2)}) copy-start(f32[1,1024,512]{2,1,0:T(8,128)} %param.21) | copy-start | bytes 6291460
  206.0 46.4 %copy-start.1 = (bf16[128,3072]{1,0:T(8,128)(2,1)S(1)}, bf16[128,3072]{1,0:T(8,128)(2,1)}, u32[]{:S(2)}) copy-start(bf16[128,3072]{1,0:T(8,128)(2,1)} %param.11) | copy-start | bytes 2359300
Sparse Core Ops, SparseCore 0:
  10.2 47.4 all-gather.5
  59.9 43.5 all-gather.3
  105.2 37.0 all-gather.7
  144.5 55.3 reduce-scatter.1
  203.3 46.9 all-reduce.1
where the time goes:
time: 259 us
  waiting for transfers between devices  140 us (54%)
  matrix products  64.3 us (25%)
  blocking collectives  36.4 us (14%)
  between operations  13.9 us (5%)
    all_gather x1, waiting for transfers between devices, shards(): lax.all_gather(x_send, 'fsdp', axis=0, tiled=True)  44.4 us
    psum x1, waiting for transfers between devices, shards(): grad_tokens = lax.psum(tok_grad.astype(jnp.bfloat16), 'exp')  39.1 us
    dot_general x5, matrix products, contract_last(): lax.dot_general(left, right, (((1,), (1,)), ((), ())), preferred_element_...  30.9 us
    all_gather x1, waiting for transfers between devices, shards(): lax.all_gather(grad_send, 'fsdp', axis=0, tiled=True)  29.5 us
    all_gather x1, blocking collectives, shards(): lax.all_gather(lowrank_grad, 'fsdp', axis=0, tiled=True)  18.4 us
    all_gather x1, blocking collectives, shards(): lax.all_gather(lowrank_tok, 'fsdp', axis=0, tiled=True)  18 us
    dot_general x1, matrix products, shards(): fwd_out = jnp.dot(x_all, fwd_matrix, preferred_element_type=jnp.float32)  16.3 us
    reduce_scatter x1, waiting for transfers between devices, shards(): lax.psum_scatter((contract_last(d_gate, gate_weight) + contract_last(d_up...  14.5 us
  transfers between devices with their start and end apart: 5, of which 5 were waited for; matrix products, arithmetic and copies ran while one was open for 24% of the time, Pallas kernels for 0%

commit v1 on v0

v1 whole, which is shorter than its diff:
```python
import jax
import jax.numpy as jnp
from jax import lax
from jax.sharding import PartitionSpec as P

momentum_decay = 0.9
grad_share = 0.1
parts_of_quarter = 2


def contract_last(left, right):
    return lax.dot_general(
        left, right, (((1,), (1,)), ((), ())), preferred_element_type=jnp.float32
    )


def contract_first(left, right):
    return lax.dot_general(
        left, right, (((0,), (0,)), ((), ())), preferred_element_type=jnp.float32
    )


def plane_swap(array, step, count):
    return lax.ppermute(array, "exp", [(i, i ^ step) for i in range(count)])


def core_swap(array, count):
    return lax.ppermute(array, "fsdp", [(i, i ^ 1) for i in range(count)])


def chip_shift(array, step, count):
    return lax.ppermute(array, "fsdp", [(i, (i + 2 * step) % count) for i in range(count)])


def routing_rows(experts_chosen, route_weight):
    rows = [experts_chosen.astype(jnp.float32).T]
    rest = route_weight.T
    for unused in range(3):
        term = lax.reduce_precision(rest, 8, 7)
        rows.append(term)
        rest = rest - term
    return jnp.concatenate(rows, axis=0).astype(jnp.bfloat16)


def read_routing(rows, experts, capacity):
    blocks, tall, tok_count = rows.shape
    top = tall // 4
    values = rows.astype(jnp.float32)
    chosen = values[:, :top]
    weight = values[:, top : 2 * top] + values[:, 2 * top : 3 * top] + values[:, 3 * top :]
    hit = chosen[:, None] == experts.astype(jnp.float32)[None, :, None, None]
    member = jnp.any(hit, axis=2)
    route = jnp.sum(jnp.where(hit, weight[:, None], 0.0), axis=2)
    before = lax.broadcasted_iota(jnp.int32, (tok_count, tok_count), 0)
    after = lax.broadcasted_iota(jnp.int32, (tok_count, tok_count), 1)
    slot = jnp.dot(
        member.astype(jnp.bfloat16).reshape(-1, tok_count),
        (before < after).astype(jnp.bfloat16),
        preferred_element_type=jnp.float32,
    ).reshape(member.shape)
    places = lax.broadcasted_iota(jnp.int32, (capacity, tok_count), 0).astype(jnp.float32)
    select = (slot[:, :, None, :] == places) & member[:, :, None, :]
    route_rows = jnp.sum(jnp.where(select, route[:, :, None, :], 0.0), axis=3)
    return select.astype(jnp.bfloat16), route_rows


def shards(
    tokens,
    out_grad,
    experts_chosen,
    route_weight,
    w_gate,
    w_up,
    w_down,
    projection,
    mom_gate,
    mom_up,
    mom_down,
):
    tok_count, width = tokens.shape
    top_count = experts_chosen.shape[1]
    count_exp = lax.axis_size("exp")
    count_fsdp = lax.axis_size("fsdp")
    chips = count_fsdp // 2
    experts_all = count_exp * w_gate.shape[0]
    capacity = min(tok_count, tok_count * top_count * 5 // (4 * experts_all))
    quarter = width // count_exp
    expert = lax.axis_index("exp")
    gate_weight = w_gate[0]
    up_weight = w_up[0]
    down_weight = w_down[0]
    bf16 = jnp.bfloat16

    steps = range(1, chips)
    own_routing = routing_rows(experts_chosen, route_weight)
    tall = own_routing.shape[0]
    start = expert * quarter
    x_part = lax.dynamic_slice_in_dim(tokens, start, quarter, 1)
    x_part = jnp.concatenate(
        [x_part, jnp.pad(own_routing, ((0, 0), (0, quarter - tok_count)))], axis=0
    )
    g_part = lax.dynamic_slice_in_dim(out_grad, start, quarter, 1)
    x_got = [chip_shift(x_part, k, count_fsdp) for k in steps]
    g_part, x_got = lax.optimization_barrier((g_part, x_got))
    g_got = [chip_shift(g_part, k, count_fsdp) for k in steps]

    order = expert ^ jnp.arange(count_exp, dtype=jnp.int32)
    rows = jnp.stack([own_routing] + [a[tok_count:, :tok_count] for a in x_got])
    select, route_rows = read_routing(rows, order, capacity)

    def pick(sel, array):
        return jnp.dot(sel, array, preferred_element_type=jnp.float32)

    def spread(whole, got, scale):
        sends = []
        for k in steps:
            picked = pick(select[k].reshape(count_exp * capacity, tok_count), got[k - 1])
            if scale:
                picked = picked * route_rows[k].reshape(-1, 1)
            sends.append(picked.astype(bf16).reshape(count_exp, capacity, quarter))
        sends = jnp.stack(sends, axis=1).reshape(count_exp, (chips - 1) * capacity, quarter)
        own = pick(select[0, 0], whole)
        if scale:
            own = own * route_rows[0, 0][:, None]
        far = jnp.zeros(((chips - 1) * capacity, width), bf16)
        for m in range(count_exp):
            piece = sends[m] if m == 0 else plane_swap(sends[m], m, count_exp)
            far = lax.dynamic_update_slice(far, piece, (0, (expert ^ m) * quarter))
        return jnp.concatenate([own.astype(bf16), far], axis=0)

    x_mine = spread(tokens, [a[:tok_count] for a in x_got], False)
    x_other = core_swap(x_mine, count_fsdp)
    grad_mine = spread(out_grad, g_got, True)
    grad_other = core_swap(grad_mine, count_fsdp)
    projection, unused = lax.optimization_barrier((projection, x_mine))
    proj_full = lax.all_gather(projection, "fsdp", axis=1, tiled=True)

    x_all = jnp.concatenate([x_mine, x_other], axis=0)
    grad_all = jnp.concatenate([grad_mine, grad_other], axis=0)
    half = chips * capacity
    gate = jnp.dot(x_all, gate_weight, preferred_element_type=jnp.float32)
    up = jnp.dot(x_all, up_weight, preferred_element_type=jnp.float32)
    sigma = jax.nn.sigmoid(gate)
    silu = gate * sigma
    hidden = (silu * up).astype(bf16)
    bwd_out = contract_last(grad_all, down_weight)
    d_gate = (bwd_out * up * sigma * (1.0 + gate * (1.0 - sigma))).astype(bf16)
    d_up = (bwd_out * silu).astype(bf16)

    sub = quarter // parts_of_quarter
    pieces = []
    for h in range(parts_of_quarter):

        def rows_of(weight):
            return weight.reshape(count_exp, parts_of_quarter, sub, -1)[:, h].reshape(
                count_exp * sub, -1
            )

        part = (
            contract_last(d_gate, rows_of(gate_weight)) + contract_last(d_up, rows_of(up_weight))
        ).astype(bf16)
        from_core = core_swap(part[half:], count_fsdp)
        summed = (part[:half].astype(jnp.float32) + from_core.astype(jnp.float32)).astype(bf16)
        came = []
        for m in range(count_exp):
            piece = lax.dynamic_slice_in_dim(summed, (expert ^ m) * sub, sub, 1)
            if m:
                piece = plane_swap(piece, m, count_exp)
            came.append(piece.reshape(chips, capacity, sub))
        came = jnp.stack(came, axis=1).reshape(chips, count_exp * capacity, sub)
        total = jnp.zeros((tok_count, sub), jnp.float32)
        for k in range(chips):
            back = contract_first(select[k].reshape(count_exp * capacity, tok_count), came[k])
            if k:
                back = chip_shift(back.astype(bf16), chips - k, count_fsdp).astype(jnp.float32)
            total = total + back
        pieces.append(total.astype(bf16))

    grad_tokens = jnp.zeros((tok_count, width), bf16)
    for h, piece in enumerate(pieces):
        for m in range(count_exp):
            got = piece if m == 0 else plane_swap(piece, m, count_exp)
            grad_tokens = lax.dynamic_update_slice(
                grad_tokens, got, (0, (expert ^ m) * quarter + h * sub)
            )

    low_tokens = contract_last(x_all, proj_full).astype(bf16)
    low_grad = contract_last(grad_all, proj_full).astype(bf16)
    new_gate = momentum_decay * mom_gate + grad_share * contract_first(low_tokens, d_gate)[None]
    new_up = momentum_decay * mom_up + grad_share * contract_first(low_tokens, d_up)[None]
    new_down = momentum_decay * mom_down + grad_share * contract_first(hidden, low_grad)[None]
    return (grad_tokens, new_gate, new_up, new_down)


def solution(mesh):
    in_specs = (
        P("fsdp", None),
        P("fsdp", None),
        P("fsdp", None),
        P("fsdp", None),
        P("exp", None, "fsdp"),
        P("exp", None, "fsdp"),
        P("exp", "fsdp", None),
        P(None, "fsdp"),
        P("exp", None, "fsdp"),
        P("exp", None, "fsdp"),
        P("exp", "fsdp", None),
    )
    out_specs = (
        P("fsdp", None),
        P("exp", None, "fsdp"),
        P("exp", None, "fsdp"),
        P("exp", "fsdp", None),
    )
    return jax.shard_map(shards, mesh=mesh, in_specs=in_specs, out_specs=out_specs, check_vma=False)
```

time: 259 us -> 205 us (0.79)
  waiting for transfers between devices: 140 us -> 44.7 us
  starting transfers between devices: 0.2 us -> 45.4 us
  blocking collectives: 36.4 us -> 0 us
  local copies, waits for them, and re-layouts: 2.24 us -> 27.9 us
  other arithmetic: 1.76 us -> 9.26 us
    all_gather x2 -> x0, waiting for transfers between devices: 73.9 us -> none  [the longest x1 44.4 us: shards(): lax.all_gather(x_send, 'fsdp', axis=0, tiled=True)]
    ppermute x0 -> x34, starting transfers between devices: none -> 45.4 us  [the longest x18 24.1 us: plane_swap(): return lax.ppermute(array, 'exp', [(i, i ^ step) for i in range(count)])]
    ppermute x0 -> x34, waiting for transfers between devices: none -> 44.7 us  [the longest x18 42.5 us: plane_swap(): return lax.ppermute(array, 'exp', [(i, i ^ step) for i in range(count)])]
    psum x1 -> x0, waiting for transfers between devices: 39.1 us -> none  [shards(): grad_tokens = lax.psum(tok_grad.astype(jnp.bfloat16), 'exp')]
    all_gather x2 -> x0, blocking collectives: 36.4 us -> none  [the longest x1 18.4 us: shards(): lax.all_gather(lowrank_grad, 'fsdp', axis=0, tiled=True)]
    reduce_scatter x1 -> x0, waiting for transfers between devices: 14.5 us -> none  [shards(): lax.psum_scatter((contract_last(d_gate, gate_weight) + contract_last(d_up...]
    slice x0 -> x8, local copies, waits for them, and re-layouts: none -> 14.4 us  [the longest x2 10.3 us: rows_of(): weight.reshape(count_exp, parts_of_quarter, sub, -1)[:, h]]
    all_gather x1, waiting for transfers between devices: 11.9 us -> 0.01 us  [shards(): proj_full = lax.all_gather(projection, 'fsdp', axis=1, tiled=True)]
  transfers between devices with their start and end apart: 5 -> 35, of which waited for: 5 -> 16; matrix products, arithmetic and copies ran while one was open for 24% -> 37% of each run, Pallas kernels for 0% -> 0%
where the time goes in v1:
time: 205 us; the launch traced here: 204 us
  matrix products  62.3 us (30%)
  starting transfers between devices  45.4 us (22%)
  waiting for transfers between devices  44.7 us (22%)
  local copies, waits for them, and re-layouts  27.9 us (14%)
  between operations  14.7 us (7%)
  other arithmetic  9.26 us (5%)
    ppermute x18, waiting for transfers between devices, plane_swap(): return lax.ppermute(array, 'exp', [(i, i ^ step) for i in range(count)])  42.5 us
    ppermute x18, starting transfers between devices, plane_swap(): return lax.ppermute(array, 'exp', [(i, i ^ step) for i in range(count)])  24.1 us
    dot_general x6, matrix products, contract_last(): lax.dot_general(left, right, (((1,), (1,)), ((), ())), preferred_element_...  22.8 us
    ppermute x12, starting transfers between devices, chip_shift(): lax.ppermute(array, 'fsdp', [(i, (i + 2 * step) % count) for i in range(c...  20.7 us
    dot_general x11, matrix products, contract_first(): lax.dot_general(left, right, (((0,), (0,)), ((), ())), preferred_element_...  16.6 us
    slice x2, local copies, waits for them, and re-layouts, rows_of(): weight.reshape(count_exp, parts_of_quarter, sub, -1)[:, h]  10.3 us
    dot_general x1, matrix products, shards(): up = jnp.dot(x_all, up_weight, preferred_element_type=jnp.float32)  9.34 us
    dot_general x1, matrix products, shards(): gate = jnp.dot(x_all, gate_weight, preferred_element_type=jnp.float32)  7.52 us
  transfers between devices with their start and end apart: 35, of which 16 were waited for; matrix products, arithmetic and copies ran while one was open for 37% of the time, Pallas kernels for 0%

profile of v1, /device:TPU:0, one launch (start us, length us, event | category | flops | bytes accessed | tf_op | source)
XLA Modules:
  0.0 204.3 jit_solution(10805434127081498418)
XLA Ops:
  8.7 3.1 %collective-permute-start = (bf16[136,768]{1,0:T(8,128)(2,1)S(1)}, bf16[136,768]{1,0:T(8,128)(2,1)}, u32[]{:S(2)}, u32[]{:S(2)}) collective-permute-start(bf16[136,768]{1,0:T(8,128)(2,1)S(1)} %pad_maximum_fusion.14), channel_id=1, source_target_pairs={{0,2},{1,3},{2,4},{3,5},{4,6},{5,7},{6,0},{7,1},{8,10},{9,11},{10,... | collective-permute-start | bytes 626696 | tf_op jit(solution)/shard_map/ppermute | solution.py:32
  11.8 2.6 %collective-permute-start.1 = (bf16[136,768]{1,0:T(8,128)(2,1)S(1)}, bf16[136,768]{1,0:T(8,128)(2,1)S(1)}, u32[]{:S(2)}, u32[]{:S(2)}) collective-permute-start(bf16[136,768]{1,0:T(8,128)(2,1)S(1)} %pad_maximum_fusion.14), channel_id=1, source_target_pairs={{0,4},{1,5},{2,6},{3,7},{4,0},{5,1},{6,2},{7,3},{8,12},{9,13},{10,... | collective-permute-start | bytes 626696 | tf_op jit(solution)/shard_map/ppermute | solution.py:32
  14.4 1.3 collective-permute-start.2
  15.8 6.4 %fusion.63 = (bf16[4,1,384,1024]{3,2,1,0:T(8,128)(2,1)}, bf16[4,1,384,1024]{3,2,1,0:T(8,128)(2,1)}) fusion(bf16[4,2,384,1024]{3,2,1,0:T(8,128)(2,1)} %bitcast.230), kind=kLoop, calls=%fused_computation.153 | loop fusion | bytes 12582912 | tf_op jit(solution)/shard_map/slice | solution.py:155
  22.2 3.9 %fusion.62 = (bf16[4,1,384,1024]{3,2,1,0:T(8,128)(2,1)}, bf16[4,1,384,1024]{3,2,1,0:T(8,128)(2,1)}) fusion(bf16[4,2,384,1024]{3,2,1,0:T(8,128)(2,1)S(1)} %bitcast.229), kind=kLoop, calls=%fused_computation.152 | loop fusion | bytes 12582912 | tf_op jit(solution)/shard_map/slice | solution.py:155
  26.1 1.6 constant_dynamic-slice_fusion.9
  28.1 4.9 %collective-permute-start.3 = (bf16[128,768]{1,0:T(8,128)(2,1)}, bf16[128,768]{1,0:T(8,128)(2,1)}, u32[]{:S(2)}, u32[]{:S(2)}) collective-permute-start(bf16[128,768]{1,0:T(8,128)(2,1)} %constant_dynamic-slice_fusion.9), channel_id=1, source_target_pairs={{0,2},{1,3},{2,4},{3,5},{4,6},{5,7},{6,0},{7,1},{8,10},{9,11},{10,... | collective-permute-start | bytes 589832 | tf_op jit(solution)/shard_map/ppermute | solution.py:32
  33.1 1.6 collective-permute-start.4
  40.4 1.5 collective-permute-start.10
  41.8 1.5 collective-permute-start.11
  45.5 6.7 %collective-permute-done.10 = bf16[240,768]{1,0:T(8,128)(2,1)} collective-permute-done((bf16[240,768]{1,0:T(8,128)(2,1)}, bf16[240,768]{1,0:T(8,128)(2,1)}, u32[]{:S(2)}, u32[]{:S(2)}) %collective-permute-start.10) | collective-permute-done | bytes 368672 | tf_op jit(solution)/shard_map/ppermute | solution.py:24
  53.2 6.4 %collective-permute-done.11 = bf16[240,768]{1,0:T(8,128)(2,1)S(1)} collective-permute-done((bf16[240,768]{1,0:T(8,128)(2,1)}, bf16[240,768]{1,0:T(8,128)(2,1)S(1)}, u32[]{:S(2)}, u32[]{:S(2)}) %collective-permute-start.11) | collective-permute-done | bytes 368672 | tf_op jit(solution)/shard_map/ppermute | solution.py:24
  59.7 1.4 pad_maximum_fusion.3
  66.8 1.4 collective-permute-start.8
  70.7 5.8 %collective-permute-done.6 = bf16[240,768]{1,0:T(8,128)(2,1)} collective-permute-done((bf16[240,768]{1,0:T(8,128)(2,1)}, bf16[240,768]{1,0:T(8,128)(2,1)}, u32[]{:S(2)}, u32[]{:S(2)}) %collective-permute-start.6) | collective-permute-done | bytes 368672 | tf_op jit(solution)/shard_map/ppermute | solution.py:24
  76.5 1.8 constant_dynamic-update-slice_fusion.14
  78.2 5.1 %collective-permute-done.7 = bf16[240,768]{1,0:T(8,128)(2,1)} collective-permute-done((bf16[240,768]{1,0:T(8,128)(2,1)}, bf16[240,768]{1,0:T(8,128)(2,1)}, u32[]{:S(2)}, u32[]{:S(2)}) %collective-permute-start.7) | collective-permute-done | bytes 368672 | tf_op jit(solution)/shard_map/ppermute | solution.py:24
  83.3 1.8 constant_dynamic-update-slice_fusion.13
  85.9 1.6 pad_maximum_fusion.2
  87.7 9.3 %fusion.2 = f32[640,1024]{1,0:T(8,128)} fusion(bf16[1,3072,1024]{2,1,0:T(8,128)(2,1)} %param.16, bf16[320,3072]{1,0:T(8,128)(2,1)} %collective-permute-done.13, bf16[240,3072]{1,0:T(8,128)(2,1)S(1)} %constant_dynamic-update-slice_fusion.8, bf16[80,3072]{1,0:T(8,128)(2,1)S(1)} %convolution_convert_fusion), kind=kOutput, calls=%fused_computation.2 | convolution fusion | flops 4038328320 | bytes 12845056 | tf_op jit(solution)/shard_map/dot_general | solution.py:142
  97.0 7.5 %fusion = f32[640,1024]{1,0:T(8,128)} fusion(bf16[1,3072,1024]{2,1,0:T(8,128)(2,1)S(1)} %bitcast.232, bf16[320,3072]{1,0:T(8,128)(2,1)} %collective-permute-done.13, bf16[240,3072]{1,0:T(8,128)(2,1)S(1)} %constant_dynamic-update-slice_fusion.8, bf16[80,3072]{1,0:T(8,128)(2,1)S(1)} %convolution_convert_fusion), kind=kOutput, calls=%fused_computation | convolution fusion | flops 4038328320 | bytes 12845056 | tf_op jit(solution)/shard_map/dot_general | solution.py:141
  104.6 9.0 %multiply_convert_fusion.1 = (bf16[640,1024]{1,0:T(8,128)(2,1)S(1)}, bf16[640,1024]{1,0:T(8,128)(2,1)S(1)}) fusion(f32[640,1024]{1,0:T(8,128)} %fusion, f32[640,1024]{1,0:T(8,128)} %fusion.2, bf16[1,1024,3072]{2,1,0:T(8,128)(2,1)S(1)} %bitcast.263, bf16[320,3072]{1,0:T(8,128)(2,1)} %collective-permute-done.9, ...), kind=kOutput, calls=%fused_computation.14 | convolution fusion | flops 4046848000 | bytes 18087936 | tf_op jit(solution)/shard_map/dot_general | solution.py:12
  113.6 2.2 %fusion.68 = f32[640,1536]{1,0:T(8,128)S(1)} fusion(bf16[640,1024]{1,0:T(8,128)(2,1)S(1)} %get-tuple-element.19, bf16[1536,1024]{1,0:T(8,128)(2,1)S(1)} %bitcast.235), kind=kOutput, calls=%fused_computation.158 | convolution fusion | flops 2013265920 | bytes 8388608 | tf_op jit(solution)/shard_map/dot_general | solution.py:12
  116.4 2.3 %add_convert_fusion.1 = bf16[640,1536]{1,0:T(8,128)(2,1)S(1)} fusion(f32[640,1536]{1,0:T(8,128)S(1)} %fusion.68, bf16[640,1024]{1,0:T(8,128)(2,1)S(1)} %get-tuple-element.18, bf16[1536,1024]{1,0:T(8,128)(2,1)S(1)} %bitcast.236), kind=kOutput, calls=%fused_computation.9 | convolution fusion | flops 2015232000 | bytes 10354688 | tf_op jit(solution)/shard_map/dot_general | solution.py:12
  118.7 2.2 %fusion.69 = f32[640,1536]{1,0:T(8,128)S(1)} fusion(bf16[640,1024]{1,0:T(8,128)(2,1)S(1)} %get-tuple-element.19, bf16[1536,1024]{1,0:T(8,128)(2,1)S(1)} %bitcast.234), kind=kOutput, calls=%fused_computation.159 | convolution fusion | flops 2013265920 | bytes 8388608 | tf_op jit(solution)/shard_map/dot_general | solution.py:12
  122.4 2.3 %add_convert_fusion = bf16[640,1536]{1,0:T(8,128)(2,1)S(1)} fusion(f32[640,1536]{1,0:T(8,128)S(1)} %fusion.69, bf16[640,1024]{1,0:T(8,128)(2,1)S(1)} %get-tuple-element.18, bf16[1536,1024]{1,0:T(8,128)(2,1)S(1)} %bitcast.233), kind=kOutput, calls=%fused_computation.8 | convolution fusion | flops 2015232000 | bytes 10354688 | tf_op jit(solution)/shard_map/dot_general | solution.py:12
  127.1 1.9 add_convert_fusion.3
  129.1 2.6 %collective-permute-start.15 = (bf16[320,384]{1,0:T(8,128)(2,1)S(1)}, bf16[320,384]{1,0:T(8,128)(2,1)S(1)}, u32[]{:S(2)}, u32[]{:S(2)}) collective-permute-start(bf16[320,384]{1,0:T(8,128)(2,1)S(1)} %get-tuple-element.35), channel_id=1, source_target_pairs={{0,8},{8,0},{16,24},{24,16},{1,9},{9,1},{17,25},{25,17},{2,10},{10... | collective-permute-start | bytes 737288 | tf_op jit(solution)/shard_map/ppermute | solution.py:24
  131.6 1.5 collective-permute-start.16
  133.2 1.4 add_convert_fusion.2
  134.8 2.0 collective-permute-start.25
  136.8 1.5 collective-permute-start.26
  138.5 2.9 %collective-permute-start.27 = (bf16[320,384]{1,0:T(8,128)(2,1)S(1)}, bf16[320,384]{1,0:T(8,128)(2,1)S(1)}, u32[]{:S(2)}, u32[]{:S(2)}) collective-permute-start(bf16[320,384]{1,0:T(8,128)(2,1)S(1)} %get-tuple-element.29), channel_id=1, source_target_pairs={{0,24},{8,16},{16,8},{24,0},{1,25},{9,17},{17,9},{25,1},{2,26},{10... | collective-permute-start | bytes 737288 | tf_op jit(solution)/shard_map/ppermute | solution.py:24
  141.4 4.4 %collective-permute-done.16 = bf16[320,384]{1,0:T(8,128)(2,1)S(1)} collective-permute-done((bf16[320,384]{1,0:T(8,128)(2,1)S(1)}, bf16[320,384]{1,0:T(8,128)(2,1)S(1)}, u32[]{:S(2)}, u32[]{:S(2)}) %collective-permute-start.16) | collective-permute-done | bytes 245792 | tf_op jit(solution)/shard_map/ppermute | solution.py:24
  146.5 2.0 collective-permute-start.18
  149.7 5.8 %collective-permute-done.26 = bf16[320,384]{1,0:T(8,128)(2,1)S(1)} collective-permute-done((bf16[320,384]{1,0:T(8,128)(2,1)S(1)}, bf16[320,384]{1,0:T(8,128)(2,1)S(1)}, u32[]{:S(2)}, u32[]{:S(2)}) %collective-permute-start.26) | collective-permute-done | bytes 245792 | tf_op jit(solution)/shard_map/ppermute | solution.py:24
  158.8 1.6 collective-permute-start.28
  160.7 1.9 collective-permute-start.30
  163.1 1.5 collective-permute-start.23
  164.6 2.6 %collective-permute-done.22 = bf16[128,384]{1,0:T(8,128)(2,1)S(1)} collective-permute-done((bf16[128,384]{1,0:T(8,128)(2,1)S(1)}, bf16[128,384]{1,0:T(8,128)(2,1)S(1)}, u32[]{:S(2)}, u32[]{:S(2)}) %collective-permute-start.22) | collective-permute-done | bytes 98336 | tf_op jit(solution)/shard_map/ppermute | solution.py:24
  167.3 1.4 collective-permute-done.23
  170.5 1.3 collective-permute-start.32
  171.8 1.5 collective-permute-start.33
  173.4 2.1 %collective-permute-done.31 = bf16[128,384]{1,0:T(8,128)(2,1)S(1)} collective-permute-done((bf16[128,384]{1,0:T(8,128)(2,1)S(1)}, bf16[128,384]{1,0:T(8,128)(2,1)S(1)}, u32[]{:S(2)}, u32[]{:S(2)}) %collective-permute-start.31) | collective-permute-done | bytes 98336 | tf_op jit(solution)/shard_map/ppermute | solution.py:24
  178.3 4.9 %convolution_convert_fusion.1 = bf16[640,512]{1,0:T(8,128)(2,1)S(1)} fusion(bf16[512,3072]{1,0:T(8,128)(2,1)} %all-gather.2.cloned.1.call-done, bf16[320,3072]{1,0:T(8,128)(2,1)} %collective-permute-done.13, bf16[240,3072]{1,0:T(8,128)(2,1)S(1)} %constant_dynamic-update-slice_fusion.8, bf16[80,3072]{1,0:T(8,128)(2,1)S(1)} %convolution_convert_fusion), kind=kOutput, calls=%fused_computation.32 | convolution fusion | flops 2025390080 | bytes 7733248 | tf_op jit(solution)/shard_map/dot_general | solution.py:12
  183.2 2.4 %bitcast_add_fusion.1 = f32[1,512,1024]{2,1,0:T(8,128)} fusion(f32[1,512,1024]{2,1,0:T(8,128)S(1)} %copy-done.6, bf16[640,512]{1,0:T(8,128)(2,1)S(1)} %convolution_convert_fusion.1, bf16[640,1024]{1,0:T(8,128)(2,1)S(1)} %copy-done.14), kind=kOutput, calls=%fused_computation.19 | convolution fusion | flops 672661504 | bytes 6160384 | tf_op jit(solution)/shard_map/dot_general | solution.py:18
  185.5 2.4 %bitcast_add_fusion.2 = f32[1,512,1024]{2,1,0:T(8,128)} fusion(f32[1,512,1024]{2,1,0:T(8,128)S(1)} %copy-done.7, bf16[640,512]{1,0:T(8,128)(2,1)S(1)} %convolution_convert_fusion.1, bf16[640,1024]{1,0:T(8,128)(2,1)S(1)} %copy-done.12), kind=kOutput, calls=%fused_computation.20 | convolution fusion | flops 672661504 | bytes 6160384 | tf_op jit(solution)/shard_map/dot_general | solution.py:18
  187.9 9.5 %bitcast_add_fusion = f32[1,1024,512]{2,1,0:T(8,128)} fusion(f32[1,1024,512]{2,1,0:T(8,128)} %param.21, f32[640,1024]{1,0:T(8,128)} %fusion.2, bf16[512,3072]{1,0:T(8,128)(2,1)} %all-gather.2.cloned.1.call-done, bf16[320,3072]{1,0:T(8,128)(2,1)} %collective-permute-done.9, bf16[240,3072]{1,0:T(8,128)(2,1)} %constant_dynamic-update-slice_fusion.12, ...), kind=kOutput, calls=%fused_computation.18 | convolution fusion | flops 2701983744 | bytes 16515072 | tf_op jit(solution)/shard_map/dot_general | solution.py:18
  (163 shorter events, 35.3 us)
Async XLA Ops:
  7.2 171.1 %all-gather.2.cloned.1.call-start = ((), (), s32[]{:S(2)}) async-start(), calls=%async_computation | async-start | bytes 3538944 | tf_op jit(solution)/shard_map/all_gather | solution.py:136
  8.7 13.4 %slice-start = ((s8[6291456]{0:T(1024)(128)(4,1)}), s8[2097152]{0:T(1024)(128)(4,1)S(1)}, s32[]{:S(2)}) async-start(s8[6291456]{0:T(1024)(128)(4,1)} %bitcast.227), calls=%async_computation.1 | async-start | bytes 4194304
  8.7 19.0 %collective-permute-start = (bf16[136,768]{1,0:T(8,128)(2,1)S(1)}, bf16[136,768]{1,0:T(8,128)(2,1)}, u32[]{:S(2)}, u32[]{:S(2)}) collective-permute-start(bf16[136,768]{1,0:T(8,128)(2,1)S(1)} %pad_maximum_fusion.14), channel_id=1, source_target_pairs={{0,2},{1,3},{2,4},{3,5},{4,6},{5,7},{6,0},{7,1},{8,10},{9,11},{10,... | collective-permute-start | bytes 626696 | tf_op jit(solution)/shard_map/ppermute | solution.py:32
  11.8 16.3 %collective-permute-start.1 = (bf16[136,768]{1,0:T(8,128)(2,1)S(1)}, bf16[136,768]{1,0:T(8,128)(2,1)S(1)}, u32[]{:S(2)}, u32[]{:S(2)}) collective-permute-start(bf16[136,768]{1,0:T(8,128)(2,1)S(1)} %pad_maximum_fusion.14), channel_id=1, source_target_pairs={{0,4},{1,5},{2,6},{3,7},{4,0},{5,1},{6,2},{7,3},{8,12},{9,13},{10,... | collective-permute-start | bytes 626696 | tf_op jit(solution)/shard_map/ppermute | solution.py:32
  14.4 13.7 %collective-permute-start.2 = (bf16[136,768]{1,0:T(8,128)(2,1)S(1)}, bf16[136,768]{1,0:T(8,128)(2,1)S(1)}, u32[]{:S(2)}, u32[]{:S(2)}) collective-permute-start(bf16[136,768]{1,0:T(8,128)(2,1)S(1)} %pad_maximum_fusion.14), channel_id=1, source_target_pairs={{0,6},{1,7},{2,0},{3,1},{4,2},{5,3},{6,4},{7,5},{8,14},{9,15},{10,... | collective-permute-start | bytes 626696 | tf_op jit(solution)/shard_map/ppermute | solution.py:32
  15.8 6.4 %slice-start.1 = ((s8[6291456]{0:T(1024)(128)(4,1)}), s8[4194304]{0:T(1024)(128)(4,1)S(1)}, s32[]{:S(2)}) async-start(s8[6291456]{0:T(1024)(128)(4,1)} %bitcast.227), calls=%async_computation.2 | async-start | bytes 8388608
  28.1 8.1 %copy-start.17 = (bf16[136,768]{1,0:T(8,128)(2,1)}, bf16[136,768]{1,0:T(8,128)(2,1)S(1)}, u32[]{:S(2)}) copy-start(bf16[136,768]{1,0:T(8,128)(2,1)S(1)} %collective-permute-done.1) | copy-start | bytes 626692
  28.1 8.1 %copy-start.19 = (bf16[136,768]{1,0:T(8,128)(2,1)}, bf16[136,768]{1,0:T(8,128)(2,1)S(1)}, u32[]{:S(2)}) copy-start(bf16[136,768]{1,0:T(8,128)(2,1)S(1)} %collective-permute-done.2) | copy-start | bytes 626692
  28.1 15.7 %collective-permute-start.3 = (bf16[128,768]{1,0:T(8,128)(2,1)}, bf16[128,768]{1,0:T(8,128)(2,1)}, u32[]{:S(2)}, u32[]{:S(2)}) collective-permute-start(bf16[128,768]{1,0:T(8,128)(2,1)} %constant_dynamic-slice_fusion.9), channel_id=1, source_target_pairs={{0,2},{1,3},{2,4},{3,5},{4,6},{5,7},{6,0},{7,1},{8,10},{9,11},{10,... | collective-permute-start | bytes 589832 | tf_op jit(solution)/shard_map/ppermute | solution.py:32
  33.1 28.1 %collective-permute-start.4 = (bf16[128,768]{1,0:T(8,128)(2,1)}, bf16[128,768]{1,0:T(8,128)(2,1)}, u32[]{:S(2)}, u32[]{:S(2)}) collective-permute-start(bf16[128,768]{1,0:T(8,128)(2,1)} %constant_dynamic-slice_fusion.9), channel_id=1, source_target_pairs={{0,4},{1,5},{2,6},{3,7},{4,0},{5,1},{6,2},{7,3},{8,12},{9,13},{10,... | collective-permute-start | bytes 589832 | tf_op jit(solution)/shard_map/ppermute | solution.py:32
  34.7 27.7 %collective-permute-start.5 = (bf16[128,768]{1,0:T(8,128)(2,1)}, bf16[128,768]{1,0:T(8,128)(2,1)}, u32[]{:S(2)}, u32[]{:S(2)}) collective-permute-start(bf16[128,768]{1,0:T(8,128)(2,1)} %constant_dynamic-slice_fusion.9), channel_id=1, source_target_pairs={{0,6},{1,7},{2,0},{3,1},{4,2},{5,3},{6,4},{7,5},{8,14},{9,15},{10,... | collective-permute-start | bytes 589832 | tf_op jit(solution)/shard_map/ppermute | solution.py:32
  40.4 11.8 %collective-permute-start.10 = (bf16[240,768]{1,0:T(8,128)(2,1)}, bf16[240,768]{1,0:T(8,128)(2,1)}, u32[]{:S(2)}, u32[]{:S(2)}) collective-permute-start(bf16[240,768]{1,0:T(8,128)(2,1)} %bitcast.28), channel_id=1, source_target_pairs={{0,8},{8,0},{16,24},{24,16},{1,9},{9,1},{17,25},{25,17},{2,10},{10... | collective-permute-start | bytes 1105928 | tf_op jit(solution)/shard_map/ppermute | solution.py:24
  41.8 17.8 %collective-permute-start.11 = (bf16[240,768]{1,0:T(8,128)(2,1)}, bf16[240,768]{1,0:T(8,128)(2,1)S(1)}, u32[]{:S(2)}, u32[]{:S(2)}) collective-permute-start(bf16[240,768]{1,0:T(8,128)(2,1)} %bitcast.29), channel_id=1, source_target_pairs={{0,16},{8,24},{16,0},{24,8},{1,17},{9,25},{17,1},{25,9},{2,18},{10... | collective-permute-start | bytes 1105928 | tf_op jit(solution)/shard_map/ppermute | solution.py:24
  43.8 15.8 %collective-permute-start.12 = (bf16[240,768]{1,0:T(8,128)(2,1)}, bf16[240,768]{1,0:T(8,128)(2,1)S(1)}, u32[]{:S(2)}, u32[]{:S(2)}) collective-permute-start(bf16[240,768]{1,0:T(8,128)(2,1)} %bitcast.30), channel_id=1, source_target_pairs={{0,24},{8,16},{16,8},{24,0},{1,25},{9,17},{17,9},{25,1},{2,26},{10... | collective-permute-start | bytes 1105928 | tf_op jit(solution)/shard_map/ppermute | solution.py:24
  61.1 26.5 %collective-permute-start.13 = (bf16[320,3072]{1,0:T(8,128)(2,1)}, bf16[320,3072]{1,0:T(8,128)(2,1)}, u32[]{:S(2)}, u32[]{:S(2)}) collective-permute-start(bf16[320,3072]{1,0:T(8,128)(2,1)} %pad_maximum_fusion.3), channel_id=1, source_target_pairs={{0,1},{1,0},{2,3},{3,2},{4,5},{5,4},{6,7},{7,6},{8,9},{9,8},{10,11... | collective-permute-start | bytes 5898248 | tf_op jit(solution)/shard_map/ppermute | solution.py:28
  64.8 11.7 %collective-permute-start.6 = (bf16[240,768]{1,0:T(8,128)(2,1)}, bf16[240,768]{1,0:T(8,128)(2,1)}, u32[]{:S(2)}, u32[]{:S(2)}) collective-permute-start(bf16[240,768]{1,0:T(8,128)(2,1)} %bitcast.20), channel_id=1, source_target_pairs={{0,8},{8,0},{16,24},{24,16},{1,9},{9,1},{17,25},{25,17},{2,10},{10... | collective-permute-start | bytes 1105928 | tf_op jit(solution)/shard_map/ppermute | solution.py:24
  65.9 17.4 %collective-permute-start.7 = (bf16[240,768]{1,0:T(8,128)(2,1)}, bf16[240,768]{1,0:T(8,128)(2,1)}, u32[]{:S(2)}, u32[]{:S(2)}) collective-permute-start(bf16[240,768]{1,0:T(8,128)(2,1)} %bitcast.21), channel_id=1, source_target_pairs={{0,16},{8,24},{16,0},{24,8},{1,17},{9,25},{17,1},{25,9},{2,18},{10... | collective-permute-start | bytes 1105928 | tf_op jit(solution)/shard_map/ppermute | solution.py:24
  66.8 18.2 %collective-permute-start.8 = (bf16[240,768]{1,0:T(8,128)(2,1)}, bf16[240,768]{1,0:T(8,128)(2,1)S(1)}, u32[]{:S(2)}, u32[]{:S(2)}) collective-permute-start(bf16[240,768]{1,0:T(8,128)(2,1)} %bitcast.22), channel_id=1, source_target_pairs={{0,24},{8,16},{16,8},{24,0},{1,25},{9,17},{17,9},{25,1},{2,26},{10... | collective-permute-start | bytes 1105928 | tf_op jit(solution)/shard_map/ppermute | solution.py:24
  85.9 11.1 %slice-start.2 = ((s8[6291456]{0:T(1024)(128)(4,1)}), s8[4194304]{0:T(1024)(128)(4,1)S(1)}, s32[]{:S(2)}) async-start(s8[6291456]{0:T(1024)(128)(4,1)} %bitcast.231), calls=%async_computation.3 | async-start | bytes 8388608
  87.5 9.5 %slice-start.3 = ((s8[6291456]{0:T(1024)(128)(4,1)}), s8[2097152]{0:T(1024)(128)(4,1)S(1)}, s32[]{:S(2)}) async-start(s8[6291456]{0:T(1024)(128)(4,1)} %bitcast.231), calls=%async_computation.4 | async-start | bytes 4194304
  87.6 17.0 %collective-permute-start.9 = (bf16[320,3072]{1,0:T(8,128)(2,1)S(1)}, bf16[320,3072]{1,0:T(8,128)(2,1)}, u32[]{:S(2)}, u32[]{:S(2)}) collective-permute-start(bf16[320,3072]{1,0:T(8,128)(2,1)S(1)} %pad_maximum_fusion.2), channel_id=1, source_target_pairs={{0,1},{1,0},{2,3},{3,2},{4,5},{5,4},{6,7},{7,6},{8,9},{9,8},{10,11... | collective-permute-start | bytes 5898248 | tf_op jit(solution)/shard_map/ppermute | solution.py:28
  87.6 16.9 %slice-start.4 = ((s8[6291456]{0:T(1024)(128)(4,1)}), s8[4194304]{0:T(1024)(128)(4,1)S(1)}, s32[]{:S(2)}) async-start(s8[6291456]{0:T(1024)(128)(4,1)} %bitcast.262), calls=%async_computation.5 | async-start | bytes 8388608
  97.0 7.5 %slice-start.5 = ((s8[6291456]{0:T(1024)(128)(4,1)}), s8[2097152]{0:T(1024)(128)(4,1)S(1)}, s32[]{:S(2)}) async-start(s8[6291456]{0:T(1024)(128)(4,1)} %bitcast.262), calls=%async_computation.6 | async-start | bytes 4194304
  104.5 9.0 %copy-start.4 = (bf16[4,1,384,1024]{3,2,1,0:T(8,128)(2,1)S(1)}, bf16[4,1,384,1024]{3,2,1,0:T(8,128)(2,1)}, u32[]{:S(2)}) copy-start(bf16[4,1,384,1024]{3,2,1,0:T(8,128)(2,1)} %get-tuple-element.17) | copy-start | bytes 9437188
  113.5 5.2 %copy-start.11 = (bf16[640,1024]{1,0:T(8,128)(2,1)}, bf16[640,1024]{1,0:T(8,128)(2,1)S(1)}, u32[]{:S(2)}) copy-start(bf16[640,1024]{1,0:T(8,128)(2,1)S(1)} %get-tuple-element.19) | copy-start | bytes 3932164
  113.5 8.9 %copy-start.13 = (bf16[640,1024]{1,0:T(8,128)(2,1)}, bf16[640,1024]{1,0:T(8,128)(2,1)S(1)}, u32[]{:S(2)}) copy-start(bf16[640,1024]{1,0:T(8,128)(2,1)S(1)} %get-tuple-element.18) | copy-start | bytes 3932164
  122.0 5.1 %collective-permute-start.14 = (bf16[320,1536]{1,0:T(8,128)(2,1)}, bf16[320,1536]{1,0:T(8,128)(2,1)}, u32[]{:S(2)}, u32[]{:S(2)}) collective-permute-start(bf16[320,1536]{1,0:T(8,128)(2,1)} %slice.223), channel_id=1, source_target_pairs={{0,1},{1,0},{2,3},{3,2},{4,5},{5,4},{6,7},{7,6},{8,9},{9,8},{10,11... | collective-permute-start | bytes 2949128 | tf_op jit(solution)/shard_map/ppermute | solution.py:28
  127.0 6.2 %collective-permute-start.24 = (bf16[320,1536]{1,0:T(8,128)(2,1)}, bf16[320,1536]{1,0:T(8,128)(2,1)}, u32[]{:S(2)}, u32[]{:S(2)}) collective-permute-start(bf16[320,1536]{1,0:T(8,128)(2,1)} %slice.231), channel_id=1, source_target_pairs={{0,1},{1,0},{2,3},{3,2},{4,5},{5,4},{6,7},{7,6},{8,9},{9,8},{10,11... | collective-permute-start | bytes 2949128 | tf_op jit(solution)/shard_map/ppermute | solution.py:28
  127.1 6.1 %copy-start.9 = (bf16[640,1536]{1,0:T(8,128)(2,1)S(1)}, bf16[640,1536]{1,0:T(8,128)(2,1)}, u32[]{:S(2)}) copy-start(bf16[640,1536]{1,0:T(8,128)(2,1)} %copy-done.8) | copy-start | bytes 5898244
  129.1 9.4 %collective-permute-start.15 = (bf16[320,384]{1,0:T(8,128)(2,1)S(1)}, bf16[320,384]{1,0:T(8,128)(2,1)S(1)}, u32[]{:S(2)}, u32[]{:S(2)}) collective-permute-start(bf16[320,384]{1,0:T(8,128)(2,1)S(1)} %get-tuple-element.35), channel_id=1, source_target_pairs={{0,8},{8,0},{16,24},{24,16},{1,9},{9,1},{17,25},{25,17},{2,10},{10... | collective-permute-start | bytes 737288 | tf_op jit(solution)/shard_map/ppermute | solution.py:24
  131.6 14.1 %collective-permute-start.16 = (bf16[320,384]{1,0:T(8,128)(2,1)S(1)}, bf16[320,384]{1,0:T(8,128)(2,1)S(1)}, u32[]{:S(2)}, u32[]{:S(2)}) collective-permute-start(bf16[320,384]{1,0:T(8,128)(2,1)S(1)} %get-tuple-element.34), channel_id=1, source_target_pairs={{0,16},{8,24},{16,0},{24,8},{1,17},{9,25},{17,1},{25,9},{2,18},{10... | collective-permute-start | bytes 737288 | tf_op jit(solution)/shard_map/ppermute | solution.py:24
  133.2 12.6 %collective-permute-start.17 = (bf16[320,384]{1,0:T(8,128)(2,1)S(1)}, bf16[320,384]{1,0:T(8,128)(2,1)S(1)}, u32[]{:S(2)}, u32[]{:S(2)}) collective-permute-start(bf16[320,384]{1,0:T(8,128)(2,1)S(1)} %get-tuple-element.33), channel_id=1, source_target_pairs={{0,24},{8,16},{16,8},{24,0},{1,25},{9,17},{17,9},{25,1},{2,26},{10... | collective-permute-start | bytes 737288 | tf_op jit(solution)/shard_map/ppermute | solution.py:24
  134.8 14.3 %collective-permute-start.25 = (bf16[320,384]{1,0:T(8,128)(2,1)S(1)}, bf16[320,384]{1,0:T(8,128)(2,1)S(1)}, u32[]{:S(2)}, u32[]{:S(2)}) collective-permute-start(bf16[320,384]{1,0:T(8,128)(2,1)S(1)} %get-tuple-element.31), channel_id=1, source_target_pairs={{0,8},{8,0},{16,24},{24,16},{1,9},{9,1},{17,25},{25,17},{2,10},{10... | collective-permute-start | bytes 737288 | tf_op jit(solution)/shard_map/ppermute | solution.py:24
  136.8 18.7 %collective-permute-start.26 = (bf16[320,384]{1,0:T(8,128)(2,1)S(1)}, bf16[320,384]{1,0:T(8,128)(2,1)S(1)}, u32[]{:S(2)}, u32[]{:S(2)}) collective-permute-start(bf16[320,384]{1,0:T(8,128)(2,1)S(1)} %get-tuple-element.30), channel_id=1, source_target_pairs={{0,16},{8,24},{16,0},{24,8},{1,17},{9,25},{17,1},{25,9},{2,18},{10... | collective-permute-start | bytes 737288 | tf_op jit(solution)/shard_map/ppermute | solution.py:24
  138.5 17.0 %collective-permute-start.27 = (bf16[320,384]{1,0:T(8,128)(2,1)S(1)}, bf16[320,384]{1,0:T(8,128)(2,1)S(1)}, u32[]{:S(2)}, u32[]{:S(2)}) collective-permute-start(bf16[320,384]{1,0:T(8,128)(2,1)S(1)} %get-tuple-element.29), channel_id=1, source_target_pairs={{0,24},{8,16},{16,8},{24,0},{1,25},{9,17},{17,9},{25,1},{2,26},{10... | collective-permute-start | bytes 737288 | tf_op jit(solution)/shard_map/ppermute | solution.py:24
  146.5 9.7 %collective-permute-start.18 = (bf16[128,384]{1,0:T(8,128)(2,1)S(1)}, bf16[128,384]{1,0:T(8,128)(2,1)S(1)}, u32[]{:S(2)}, u32[]{:S(2)}) collective-permute-start(bf16[128,384]{1,0:T(8,128)(2,1)S(1)} %fusion.13), channel_id=1, source_target_pairs={{0,6},{1,7},{2,0},{3,1},{4,2},{5,3},{6,4},{7,5},{8,14},{9,15},{10,... | collective-permute-start | bytes 294920 | tf_op jit(solution)/shard_map/ppermute | solution.py:32
  148.4 8.7 %collective-permute-start.19 = (bf16[128,384]{1,0:T(8,128)(2,1)S(1)}, bf16[128,384]{1,0:T(8,128)(2,1)S(1)}, u32[]{:S(2)}, u32[]{:S(2)}) collective-permute-start(bf16[128,384]{1,0:T(8,128)(2,1)S(1)} %fusion.14), channel_id=1, source_target_pairs={{0,4},{1,5},{2,6},{3,7},{4,0},{5,1},{6,2},{7,3},{8,12},{9,13},{10,... | collective-permute-start | bytes 294920 | tf_op jit(solution)/shard_map/ppermute | solution.py:32
  149.0 8.1 %collective-permute-start.20 = (bf16[128,384]{1,0:T(8,128)(2,1)S(1)}, bf16[128,384]{1,0:T(8,128)(2,1)S(1)}, u32[]{:S(2)}, u32[]{:S(2)}) collective-permute-start(bf16[128,384]{1,0:T(8,128)(2,1)S(1)} %fusion.15), channel_id=1, source_target_pairs={{0,2},{1,3},{2,4},{3,5},{4,6},{5,7},{6,0},{7,1},{8,10},{9,11},{10,... | collective-permute-start | bytes 294920 | tf_op jit(solution)/shard_map/ppermute | solution.py:32
  157.5 5.6 %collective-permute-start.21 = (bf16[128,384]{1,0:T(8,128)(2,1)S(1)}, bf16[128,384]{1,0:T(8,128)(2,1)S(1)}, u32[]{:S(2)}, u32[]{:S(2)}) collective-permute-start(bf16[128,384]{1,0:T(8,128)(2,1)S(1)} %get-tuple-element.50), channel_id=1, source_target_pairs={{0,8},{8,0},{16,24},{24,16},{1,9},{9,1},{17,25},{25,17},{2,10},{10... | collective-permute-start | bytes 294920 | tf_op jit(solution)/shard_map/ppermute | solution.py:24
  158.8 9.9 %collective-permute-start.28 = (bf16[128,384]{1,0:T(8,128)(2,1)S(1)}, bf16[128,384]{1,0:T(8,128)(2,1)S(1)}, u32[]{:S(2)}, u32[]{:S(2)}) collective-permute-start(bf16[128,384]{1,0:T(8,128)(2,1)S(1)} %fusion.16), channel_id=1, source_target_pairs={{0,6},{1,7},{2,0},{3,1},{4,2},{5,3},{6,4},{7,5},{8,14},{9,15},{10,... | collective-permute-start | bytes 294920 | tf_op jit(solution)/shard_map/ppermute | solution.py:32
  160.4 9.1 %collective-permute-start.29 = (bf16[128,384]{1,0:T(8,128)(2,1)S(1)}, bf16[128,384]{1,0:T(8,128)(2,1)S(1)}, u32[]{:S(2)}, u32[]{:S(2)}) collective-permute-start(bf16[128,384]{1,0:T(8,128)(2,1)S(1)} %fusion.17), channel_id=1, source_target_pairs={{0,4},{1,5},{2,6},{3,7},{4,0},{5,1},{6,2},{7,3},{8,12},{9,13},{10,... | collective-permute-start | bytes 294920 | tf_op jit(solution)/shard_map/ppermute | solution.py:32
  160.7 8.8 %collective-permute-start.30 = (bf16[128,384]{1,0:T(8,128)(2,1)S(1)}, bf16[128,384]{1,0:T(8,128)(2,1)S(1)}, u32[]{:S(2)}, u32[]{:S(2)}) collective-permute-start(bf16[128,384]{1,0:T(8,128)(2,1)S(1)} %fusion.18), channel_id=1, source_target_pairs={{0,2},{1,3},{2,4},{3,5},{4,6},{5,7},{6,0},{7,1},{8,10},{9,11},{10,... | collective-permute-start | bytes 294920 | tf_op jit(solution)/shard_map/ppermute | solution.py:32
  162.6 4.6 %collective-permute-start.22 = (bf16[128,384]{1,0:T(8,128)(2,1)S(1)}, bf16[128,384]{1,0:T(8,128)(2,1)S(1)}, u32[]{:S(2)}, u32[]{:S(2)}) collective-permute-start(bf16[128,384]{1,0:T(8,128)(2,1)S(1)} %get-tuple-element.50), channel_id=1, source_target_pairs={{0,16},{8,24},{16,0},{24,8},{1,17},{9,25},{17,1},{25,9},{2,18},{10... | collective-permute-start | bytes 294920 | tf_op jit(solution)/shard_map/ppermute | solution.py:24
  163.1 5.5 %collective-permute-start.23 = (bf16[128,384]{1,0:T(8,128)(2,1)S(1)}, bf16[128,384]{1,0:T(8,128)(2,1)S(1)}, u32[]{:S(2)}, u32[]{:S(2)}) collective-permute-start(bf16[128,384]{1,0:T(8,128)(2,1)S(1)} %get-tuple-element.50), channel_id=1, source_target_pairs={{0,24},{8,16},{16,8},{24,0},{1,25},{9,17},{17,9},{25,1},{2,26},{10... | collective-permute-start | bytes 294920 | tf_op jit(solution)/shard_map/ppermute | solution.py:24
  169.8 5.7 %collective-permute-start.31 = (bf16[128,384]{1,0:T(8,128)(2,1)S(1)}, bf16[128,384]{1,0:T(8,128)(2,1)S(1)}, u32[]{:S(2)}, u32[]{:S(2)}) collective-permute-start(bf16[128,384]{1,0:T(8,128)(2,1)S(1)} %get-tuple-element.52), channel_id=1, source_target_pairs={{0,8},{8,0},{16,24},{24,16},{1,9},{9,1},{17,25},{25,17},{2,10},{10... | collective-permute-start | bytes 294920 | tf_op jit(solution)/shard_map/ppermute | solution.py:24
  170.5 5.7 %collective-permute-start.32 = (bf16[128,384]{1,0:T(8,128)(2,1)S(1)}, bf16[128,384]{1,0:T(8,128)(2,1)S(1)}, u32[]{:S(2)}, u32[]{:S(2)}) collective-permute-start(bf16[128,384]{1,0:T(8,128)(2,1)S(1)} %get-tuple-element.52), channel_id=1, source_target_pairs={{0,16},{8,24},{16,0},{24,8},{1,17},{9,25},{17,1},{25,9},{2,18},{10... | collective-permute-start | bytes 294920 | tf_op jit(solution)/shard_map/ppermute | solution.py:24
  171.8 5.5 %collective-permute-start.33 = (bf16[128,384]{1,0:T(8,128)(2,1)S(1)}, bf16[128,384]{1,0:T(8,128)(2,1)S(1)}, u32[]{:S(2)}, u32[]{:S(2)}) collective-permute-start(bf16[128,384]{1,0:T(8,128)(2,1)S(1)} %get-tuple-element.52), channel_id=1, source_target_pairs={{0,24},{8,16},{16,8},{24,0},{1,25},{9,17},{17,9},{25,1},{2,26},{10... | collective-permute-start | bytes 294920 | tf_op jit(solution)/shard_map/ppermute | solution.py:24
  187.9 9.5 %copy-start.1 = (bf16[128,3072]{1,0:T(8,128)(2,1)S(1)}, bf16[128,3072]{1,0:T(8,128)(2,1)}, u32[]{:S(2)}) copy-start(bf16[128,3072]{1,0:T(8,128)(2,1)} %param.11) | copy-start | bytes 2359300
  (14 other events, 39.8 us)
Sparse Core Ops, SparseCore 0:
  70.8 36.6 all-gather.1

commit v2 on v0

v2 whole, which is shorter than its diff:
```python
import functools

import jax
import jax.numpy as jnp
from jax import lax
from jax.experimental import pallas as pl
from jax.experimental.pallas import tpu as pltpu
from jax.sharding import PartitionSpec as P

momentum_decay = 0.9
grad_share = 0.1
lanes = 128
bf16 = jnp.bfloat16
f32 = jnp.float32
vmem = pl.BlockSpec(memory_space=pltpu.VMEM)
smem = pl.BlockSpec(memory_space=pltpu.SMEM)


def contract_last(left, right):
    return lax.dot_general(left, right, (((1,), (1,)), ((), ())), preferred_element_type=f32)


def contract_first(left, right):
    return lax.dot_general(left, right, (((0,), (0,)), ((), ())), preferred_element_type=f32)


def plain(left, right):
    return jnp.dot(left, right, preferred_element_type=f32)


def plane_swap(array, step, count):
    return lax.ppermute(array, "exp", [(i, i ^ step) for i in range(count)])


def core_swap(array, count):
    return lax.ppermute(array, "fsdp", [(i, i ^ 1) for i in range(count)])


def after(value, *others):
    return lax.optimization_barrier((value, others))[0]


def chip_swap(array, step, count):
    return lax.ppermute(array, "fsdp", [(i, i ^ (2 * step)) for i in range(count)])


def tile_of(size, wanted):
    return wanted if size % wanted == 0 else size


def routing_rows(experts_chosen, route_weight):
    rows = [experts_chosen.astype(f32).T]
    rest = route_weight.T
    for unused in range(3):
        term = lax.reduce_precision(rest, 8, 7)
        rows.append(term)
        rest = rest - term
    rows = jnp.concatenate(rows, axis=0)
    return jnp.pad(rows, ((0, -rows.shape[0] % 16), (0, 0))).astype(bf16)


def select_kernel(top, ids, own, *refs):
    experts = ids.shape[0]
    blocks = len(refs) - 1 - experts
    got, sends = refs[: blocks - 1], refs[blocks - 1 : blocks - 1 + experts]
    select, route_rows = refs[-2:]
    tok_count = own.shape[1]
    capacity = select.shape[1] // experts
    below = lax.broadcasted_iota(jnp.int32, (tok_count, tok_count), 0)
    right = lax.broadcasted_iota(jnp.int32, (tok_count, tok_count), 1)
    earlier = (below < right).astype(f32).astype(bf16)
    places = lax.broadcasted_iota(jnp.int32, (capacity, tok_count), 0).astype(f32)
    for k in range(blocks):
        rows = (own[...] if k == 0 else got[k - 1][tok_count : tok_count + own.shape[0], :tok_count]).astype(f32)
        chosen = rows[:top]
        weight = rows[top : 2 * top] + rows[2 * top : 3 * top] + rows[3 * top : 4 * top]
        members, routes = [], []
        for m in range(experts):
            hit = (chosen == ids[m].astype(f32)).astype(f32)
            members.append(jnp.max(hit, axis=0, keepdims=True))
            routes.append(jnp.sum(hit * weight, axis=0, keepdims=True))
        member = jnp.concatenate(members, axis=0)
        slot = plain(member.astype(bf16), earlier)
        for m in range(experts):
            here = (slot[m : m + 1] == places) & (member[m : m + 1] > 0.0)
            one = here.astype(f32)
            select[k, m * capacity : (m + 1) * capacity, :] = one.astype(bf16)
            share = jnp.sum(one * routes[m], axis=1, keepdims=True)
            route_rows[k, m * capacity : (m + 1) * capacity, :] = jnp.broadcast_to(
                share, (capacity, lanes)
            )
            if k:
                sends[m][(k - 1) * capacity : k * capacity, :] = plain(
                    one.astype(bf16), got[k - 1][:tok_count, :]
                ).astype(bf16)


def scaled_kernel(select, route_rows, *refs):
    blocks = select.shape[0]
    got, sends = refs[: blocks - 1], refs[blocks - 1 :]
    capacity = select.shape[1] // len(sends)
    for k in range(1, blocks):
        for m in range(len(sends)):
            span = slice(m * capacity, (m + 1) * capacity)
            rows = plain(select[k, span, :], got[k - 1][...]) * route_rows[k, span, :1]
            sends[m][(k - 1) * capacity : k * capacity, :] = rows.astype(bf16)


def pack_kernel(scale, starts, select, route_rows, whole, *refs):
    pieces, out = refs[:-1], refs[-1]
    experts = len(pieces)
    capacity = select.shape[1] // experts
    quarter = pieces[0].shape[1]
    own = plain(select[0, :capacity, :], whole[...])
    if scale:
        own = own * route_rows[0, :capacity, :1]
    out[:capacity, :] = own.astype(bf16)
    for m in range(experts):
        columns = pl.ds(pl.multiple_of(starts[m], lanes), quarter)
        out[capacity:, columns] = pieces[m][...]


def forward_kernel(mine, other, w_gate, w_up, *outs):
    for half, rows in enumerate((mine, other)):
        hidden, silu_out, factor_out = outs[3 * half : 3 * half + 3]
        gate = plain(rows[...], w_gate[0])
        up = plain(rows[...], w_up[0])
        sigma = jax.nn.sigmoid(gate)
        silu = gate * sigma
        hidden[...] = (silu * up).astype(bf16)
        silu_out[...] = silu.astype(bf16)
        factor_out[...] = (up * sigma * (1.0 + gate * (1.0 - sigma))).astype(bf16)


def back_kernel(grad, w_down, silu, factor, *refs):
    d_gate, d_up = refs[-2:]
    back = contract_last(grad[...], w_down[0])
    d_gate[...] = (back * factor[...].astype(f32)).astype(bf16)
    d_up[...] = (back * silu[...].astype(f32)).astype(bf16)


def merge_kernel(starts, part, more, *outs):
    half, sub = outs[0].shape
    for m, out in enumerate(outs):
        columns = pl.ds(pl.multiple_of(starts[m], lanes), sub)
        out[...] = (part[:half, columns].astype(f32) + more[:, columns].astype(f32)).astype(bf16)


def place_kernel(starts, *refs):
    pieces, out = refs[:-1], refs[-1]
    experts = starts.shape[0]
    sub = pieces[0].shape[1]
    for i, piece in enumerate(pieces):
        first = starts[i % experts] + (i // experts) * experts * sub
        out[:, pl.ds(pl.multiple_of(first, lanes), sub)] = piece[...]


def token_kernel(select, *refs):
    blocks = select.shape[0]
    came, outs = refs[:-blocks], refs[-blocks:]
    capacity = select.shape[1] // len(came)
    for k in range(blocks):
        rows = jnp.concatenate(
            [piece[k * capacity : (k + 1) * capacity, :] for piece in came], axis=0
        )
        outs[k][...] = contract_first(select[k], rows).astype(outs[k].dtype)


def low_kernel(mine, other, g_mine, g_other, projection, *outs):
    for rows, out in zip((mine, other, g_mine, g_other), outs):
        out[...] = contract_last(rows[...], projection[...]).astype(bf16)


def momentum_kernel(lt0, lt1, lg0, lg1, d_gate, d_up, h0, h1, mg, mu, md, og, ou, od):
    half = lt0.shape[0]
    for old, new, pairs in (
        (mg, og, ((lt0[...], d_gate[:half, :]), (lt1[...], d_gate[half:, :]))),
        (mu, ou, ((lt0[...], d_up[:half, :]), (lt1[...], d_up[half:, :]))),
        (md, od, ((h0[...], lg0[...]), (h1[...], lg1[...]))),
    ):
        total = contract_first(*pairs[0]) + contract_first(*pairs[1])
        new[0] = momentum_decay * old[0] + grad_share * total


def call(
    kernel, name, shapes, in_specs, out_specs, grid=(), scalars=0, limit=16, alias=None, flops=0
):
    return pl.pallas_call(
        kernel,
        name=name,
        out_shape=[jax.ShapeDtypeStruct(s, t) for s, t in shapes],
        grid_spec=pltpu.PrefetchScalarGridSpec(
            num_scalar_prefetch=scalars, grid=grid, in_specs=in_specs, out_specs=out_specs
        ),
        input_output_aliases=alias or {},
        compiler_params=pltpu.CompilerParams(vmem_limit_bytes=limit << 20),
        cost_estimate=pl.CostEstimate(flops=flops, bytes_accessed=0, transcendentals=0),
    )


def shards(
    tokens,
    out_grad,
    experts_chosen,
    route_weight,
    w_gate,
    w_up,
    w_down,
    projection,
    mom_gate,
    mom_up,
    mom_down,
):
    tok_count, width = tokens.shape
    top = experts_chosen.shape[1]
    hidden_local = w_gate.shape[2]
    rank = projection.shape[0]
    count_exp = lax.axis_size("exp")
    count_fsdp = lax.axis_size("fsdp")
    chips = count_fsdp // 2
    experts_all = count_exp * w_gate.shape[0]
    capacity = min(tok_count, tok_count * top * 5 // (4 * experts_all))
    capacity = -(-capacity // 16) * 16
    quarter = width // count_exp
    half = chips * capacity
    far = (chips - 1) * capacity
    expert = lax.axis_index("exp")
    steps = range(1, chips)
    order = expert ^ jnp.arange(count_exp, dtype=jnp.int32)
    starts = order * quarter

    own_routing = routing_rows(experts_chosen, route_weight)
    tall = own_routing.shape[0]
    start = expert * quarter
    x_part = jnp.concatenate(
        [
            lax.dynamic_slice_in_dim(tokens, start, quarter, 1),
            jnp.pad(own_routing, ((0, 0), (0, quarter - tok_count))),
        ],
        axis=0,
    )
    g_part = lax.dynamic_slice_in_dim(out_grad, start, quarter, 1)
    x_got = [chip_swap(x_part, k, count_fsdp) for k in steps]
    g_part = after(g_part, x_got)
    g_got = [chip_swap(g_part, k, count_fsdp) for k in steps]

    parts_of_quarter = next(n for n in (2, 3, 1) if quarter % (n * lanes) == 0 or n == 1)
    sub = quarter // parts_of_quarter

    send_shapes = [((far, quarter), bf16)] * count_exp
    *x_send, select, route_rows = call(
        functools.partial(select_kernel, top),
        "select",
        send_shapes
        + [
            ((chips, count_exp * capacity, tok_count), bf16),
            ((chips, count_exp * capacity, lanes), f32),
        ],
        [smem] + [vmem] * chips,
        [vmem] * (count_exp + 2),
    )(order, own_routing, *x_got)

    def gathered(send):
        return [send[0]] + [plane_swap(send[m], m, count_exp) for m in range(1, count_exp)]

    def pack(scale, whole, pieces):
        return call(
            functools.partial(pack_kernel, scale),
            "pack",
            [((half, width), bf16)],
            [smem] + [vmem] * (3 + count_exp),
            [vmem],
        )(starts, select, route_rows, whole, *pieces)[0]

    x_pieces = gathered(x_send)
    g_send = call(scaled_kernel, "scaled", send_shapes, [vmem] * (chips + 1), [vmem] * count_exp)(
        select, route_rows, *g_got
    )

    x_pieces[0] = after(x_pieces[0], g_send[0])
    x_mine = pack(False, tokens, x_pieces)
    x_other = core_swap(x_mine, count_fsdp)
    g_pieces = gathered(g_send)

    width_f = tile_of(hidden_local, 256)
    row_f = pl.BlockSpec((half, width_f), lambda i: (0, i))
    weight_f = pl.BlockSpec((1, width, width_f), lambda i: (0, 0, i))
    half_shape = ((half, hidden_local), bf16)
    h0, silu0, factor0, h1, silu1, factor1 = call(
        forward_kernel,
        "forward",
        [half_shape] * 6,
        [vmem, vmem, weight_f, weight_f],
        [row_f] * 6,
        grid=(hidden_local // width_f,),
        limit=54,
        flops=8 * half * width * hidden_local,
    )(x_mine, x_other, w_gate, w_up)

    g_pieces[0] = after(g_pieces[0], h0)
    grad_mine = pack(True, out_grad, g_pieces)
    grad_other = core_swap(grad_mine, count_fsdp)

    def backward(number, grad, silu, factor, *held):
        rows = pl.BlockSpec((half, width_f), lambda i: (number, i))
        return call(
            back_kernel,
            "backward",
            [((2 * half, hidden_local), bf16)] * 2,
            [vmem, pl.BlockSpec((1, width_f, width), lambda i: (0, i, 0)), row_f, row_f]
            + [pl.BlockSpec(memory_space=pl.ANY)] * len(held),
            [rows] * 2,
            grid=(hidden_local // width_f,),
        limit=14,
            alias={4: 0, 5: 1} if held else None,
        )(grad, w_down, silu, factor, *held)

    d_gate, d_up = backward(0, grad_mine, silu0, factor0)
    d_gate, d_up = backward(1, grad_other, silu1, factor1, d_gate, d_up)

    def part_of(h, d_gate, d_up):
        span = slice(h * count_exp * sub, (h + 1) * count_exp * sub)
        part = contract_last(d_gate, w_gate[0, span]) + contract_last(d_up, w_up[0, span])
        part = part.astype(bf16)
        return part, core_swap(part[half:], count_fsdp)

    def merge(part, from_core):
        outs = call(
            merge_kernel,
            "merge",
            [((half, sub), bf16)] * count_exp,
            [smem] + [vmem] * 2,
            [vmem] * count_exp,
        )(order * sub, part, from_core)
        return list(outs), gathered(outs)

    def to_tokens(came):
        own, *rest = call(
            token_kernel,
            "to_tokens",
            [((tok_count, sub), f32)] + [((tok_count, sub), bf16)] * (chips - 1),
            [vmem] * (1 + count_exp),
            [vmem] * chips,
        )(select, *came)
        return own, [chip_swap(rest[k - 1], k, count_fsdp) for k in steps]

    def summed(own, got):
        total = own
        for piece in got:
            total = total + piece.astype(f32)
        return gathered([total.astype(bf16)] * count_exp)

    parts = [part_of(h, d_gate, d_up) for h in range(parts_of_quarter)]
    all_came, sent = [], None
    for part, from_core in parts:
        sent, came = merge(part, from_core if sent is None else after(from_core, sent))
        all_came.append(came)
    proj_full = lax.all_gather(after(projection, g_got), "fsdp", axis=1, tiled=True)
    width_r = tile_of(rank, 256)
    low_spec = pl.BlockSpec((half, width_r), lambda i: (0, i))
    lows = call(
        low_kernel,
        "low",
        [((half, rank), bf16)] * 4,
        [vmem] * 4 + [pl.BlockSpec((width_r, width), lambda i: (i, 0))],
        [low_spec] * 4,
        grid=(rank // width_r,),
        limit=40,
    )(x_mine, x_other, grad_mine, grad_other, proj_full)
    all_came[0][0] = after(all_came[0][0], lows)
    across = pl.BlockSpec((1, rank, width_f), lambda i: (0, 0, i))
    along = pl.BlockSpec((1, width_f, rank), lambda i: (0, i, 0))
    both_f = pl.BlockSpec((2 * half, width_f), lambda i: (0, i))
    new_gate, new_up, new_down = call(
        momentum_kernel,
        "momentum",
        [(mom_gate.shape, f32), (mom_up.shape, f32), (mom_down.shape, f32)],
        [vmem] * 4 + [both_f] * 2 + [row_f] * 2 + [across, across, along],
        [across, across, along],
        grid=(hidden_local // width_f,),
        limit=20,
    )(*lows, d_gate, d_up, h0, h1, mom_gate, mom_up, mom_down)

    for came in all_came[1:]:
        came[0] = after(came[0], new_gate)
    totals = [to_tokens(came) for came in all_came]
    pieces = []
    for own, got in totals:
        pieces += summed(own, got)

    grad_tokens = call(
        place_kernel, "place", [((tok_count, width), bf16)], [smem] + [vmem] * len(pieces), [vmem]
    )(order * sub, *pieces)[0]
    return (grad_tokens, new_gate, new_up, new_down)


def solution(mesh):
    in_specs = (
        P("fsdp", None),
        P("fsdp", None),
        P("fsdp", None),
        P("fsdp", None),
        P("exp", None, "fsdp"),
        P("exp", None, "fsdp"),
        P("exp", "fsdp", None),
        P(None, "fsdp"),
        P("exp", None, "fsdp"),
        P("exp", None, "fsdp"),
        P("exp", "fsdp", None),
    )
    out_specs = (
        P("fsdp", None),
        P("exp", None, "fsdp"),
        P("exp", None, "fsdp"),
        P("exp", "fsdp", None),
    )
    return jax.shard_map(shards, mesh=mesh, in_specs=in_specs, out_specs=out_specs, check_vma=False)
```

time: 259 us -> 166 us (0.64)
  waiting for transfers between devices: 140 us -> 34.3 us
  matrix products: 64.3 us -> 8.96 us
  Pallas kernels: 0 us -> 47.9 us
  starting transfers between devices: 0.2 us -> 47.1 us
  blocking collectives: 36.4 us -> 0 us
  local copies, waits for them, and re-layouts: 2.24 us -> 11.7 us
    all_gather x3 -> x1, waiting for transfers between devices: 85.8 us -> 0.46 us  [shards(): lax.all_gather(after(projection, g_got), 'fsdp', axis=1, tiled=True)]
    pallas_call x0 -> x14, Pallas kernels: none -> 47.9 us  [the longest x1 13 us: shards(): call(forward_kernel, 'forward', [half_shape] * 6, [vmem, vmem, weight_f,...]
    ppermute x0 -> x34, starting transfers between devices: none -> 47 us  [the longest x12 24.7 us: chip_swap(): lax.ppermute(array, 'fsdp', [(i, i ^ 2 * step) for i in range(count)])]
    psum x1 -> x0, waiting for transfers between devices: 39.1 us -> none  [shards(): grad_tokens = lax.psum(tok_grad.astype(jnp.bfloat16), 'exp')]
    all_gather x2 -> x0, blocking collectives: 36.4 us -> none  [the longest x1 18.4 us: shards(): lax.all_gather(lowrank_grad, 'fsdp', axis=0, tiled=True)]
    ppermute x0 -> x34, waiting for transfers between devices: none -> 33.9 us  [the longest x12 24.1 us: chip_swap(): lax.ppermute(array, 'fsdp', [(i, i ^ 2 * step) for i in range(count)])]
    dot_general x7 -> x0, matrix products: 33.4 us -> none  [the longest x1 16.3 us: shards(): fwd_out = jnp.dot(x_all, fwd_matrix, preferred_element_type=jnp.float32)]
    dot_general x5 -> x4, matrix products: 30.9 us -> 8.96 us  [contract_last(): lax.dot_general(left, right, (((1,), (1,)), ((), ())), preferred_element_...]
  transfers between devices with their start and end apart: 5 -> 35, of which waited for: 5 -> 14; matrix products, arithmetic and copies ran while one was open for 24% -> 6% of each run, Pallas kernels for 0% -> 26%
where the time goes in v2:
time: 166 us
  Pallas kernels  47.9 us (29%)
  starting transfers between devices  47.1 us (28%)
  waiting for transfers between devices  34.3 us (21%)
  between operations  14.5 us (9%)
  local copies, waits for them, and re-layouts  11.7 us (7%)
  matrix products  8.96 us (5%)
    ppermute x12, starting transfers between devices, chip_swap(): lax.ppermute(array, 'fsdp', [(i, i ^ 2 * step) for i in range(count)])  24.7 us
    ppermute x12, waiting for transfers between devices, chip_swap(): lax.ppermute(array, 'fsdp', [(i, i ^ 2 * step) for i in range(count)])  24.1 us
    ppermute x18, starting transfers between devices, plane_swap(): return lax.ppermute(array, 'exp', [(i, i ^ step) for i in range(count)])  21.6 us
    pallas_call x1, Pallas kernels, shards(): call(forward_kernel, 'forward', [half_shape] * 6, [vmem, vmem, weight_f,...  13 us
    pallas_call x2, Pallas kernels, backward(): call(back_kernel, 'backward', [((2 * half, hidden_local), bf16)] * 2, [vm...  9.81 us
    unnamed x62, local copies, waits for them, and re-layouts  9.65 us
    ppermute x18, waiting for transfers between devices, plane_swap(): return lax.ppermute(array, 'exp', [(i, i ^ step) for i in range(count)])  9.32 us
    dot_general x4, matrix products, contract_last(): lax.dot_general(left, right, (((1,), (1,)), ((), ())), preferred_element_...  8.96 us
  transfers between devices with their start and end apart: 35, of which 14 were waited for; matrix products, arithmetic and copies ran while one was open for 6% of the time, Pallas kernels for 26%

profile of v2, /device:TPU:0, one launch (start us, length us, event | category | flops | bytes accessed | tf_op | source)
XLA Modules:
  0.0 166.0 jit_solution(18020923871590844514)
XLA Ops:
  9.6 5.1 %collective-permute-start.2 = (bf16[144,768]{1,0:T(8,128)(2,1)S(1)}, bf16[144,768]{1,0:T(8,128)(2,1)S(1)}, u32[]{:S(2)}, u32[]{:S(2)}) collective-permute-start(bf16[144,768]{1,0:T(8,128)(2,1)S(1)} %fusion.11), channel_id=1, source_target_pairs={{0,6},{1,7},{2,4},{3,5},{4,2},{5,3},{6,0},{7,1},{8,14},{9,15},{10,... | collective-permute-start | bytes 663560 | tf_op jit(solution)/shard_map/ppermute | solution.py:44
  16.3 4.8 %collective-permute-done.2.refs_2_ = bf16[144,768]{1,0:T(8,128)(2,1)S(1)} collective-permute-done((bf16[144,768]{1,0:T(8,128)(2,1)S(1)}, bf16[144,768]{1,0:T(8,128)(2,1)S(1)}, u32[]{:S(2)}, u32[]{:S(2)}) %collective-permute-start.2) | collective-permute-done | bytes 221216 | tf_op jit(solution)/shard_map/ppermute | solution.py:44
  21.2 12.4 %collective-permute-done.1.refs_1_ = bf16[144,768]{1,0:T(8,128)(2,1)S(1)} collective-permute-done((bf16[144,768]{1,0:T(8,128)(2,1)S(1)}, bf16[144,768]{1,0:T(8,128)(2,1)S(1)}, u32[]{:S(2)}, u32[]{:S(2)}) %collective-permute-start.1) | collective-permute-done | bytes 221216 | tf_op jit(solution)/shard_map/ppermute | solution.py:44
  33.6 2.7 %collective-permute-start.5 = (bf16[128,768]{1,0:T(8,128)(2,1)S(1)}, bf16[128,768]{1,0:T(8,128)(2,1)S(1)}, u32[]{:S(2)}, u32[]{:S(2)}) collective-permute-start(bf16[128,768]{1,0:T(8,128)(2,1)S(1)} %constant_dynamic-slice_fusion), channel_id=1, source_target_pairs={{0,6},{1,7},{2,4},{3,5},{4,2},{5,3},{6,0},{7,1},{8,14},{9,15},{10,... | collective-permute-start | bytes 589832 | tf_op jit(solution)/shard_map/ppermute | solution.py:44
  36.3 1.5 select.27
  37.8 1.6 collective-permute-start.6
  39.3 1.5 collective-permute-start.7
  41.4 7.4 %collective-permute-start.3 = (bf16[128,768]{1,0:T(8,128)(2,1)S(1)}, bf16[128,768]{1,0:T(8,128)(2,1)S(1)}, u32[]{:S(2)}, u32[]{:S(2)}) collective-permute-start(bf16[128,768]{1,0:T(8,128)(2,1)S(1)} %constant_dynamic-slice_fusion), channel_id=1, source_target_pairs={{0,2},{1,3},{2,0},{3,1},{4,6},{5,7},{6,4},{7,5},{8,10},{9,11},{10,... | collective-permute-start | bytes 589832 | tf_op jit(solution)/shard_map/ppermute | solution.py:44
  48.8 2.5 %collective-permute-done.4.refs_1_ = bf16[128,768]{1,0:T(8,128)(2,1)S(1)} collective-permute-done((bf16[128,768]{1,0:T(8,128)(2,1)S(1)}, bf16[128,768]{1,0:T(8,128)(2,1)S(1)}, u32[]{:S(2)}, u32[]{:S(2)}) %collective-permute-start.4) | collective-permute-done | bytes 196640 | tf_op jit(solution)/shard_map/ppermute | solution.py:44
  51.3 2.0 %collective-permute-done.3.refs_0_ = bf16[128,768]{1,0:T(8,128)(2,1)S(1)} collective-permute-done((bf16[128,768]{1,0:T(8,128)(2,1)S(1)}, bf16[128,768]{1,0:T(8,128)(2,1)S(1)}, u32[]{:S(2)}, u32[]{:S(2)}) %collective-permute-start.3) | collective-permute-done | bytes 196640 | tf_op jit(solution)/shard_map/ppermute | solution.py:44
  53.8 2.1 %collective-permute-done.7.refs_2_ = bf16[240,768]{1,0:T(8,128)(2,1)S(1)} collective-permute-done((bf16[240,768]{1,0:T(8,128)(2,1)S(1)}, bf16[240,768]{1,0:T(8,128)(2,1)S(1)}, u32[]{:S(2)}, u32[]{:S(2)}) %collective-permute-start.7) | collective-permute-done | bytes 368672 | tf_op jit(solution)/shard_map/ppermute | solution.py:32
  55.9 1.0 pack.2.mine
  57.0 1.3 collective-permute-start.10
  59.1 1.4 collective-permute-start.12
  61.0 1.3 copy-done.11
  62.2 13.0 %forward.1 = (bf16[320,1024]{1,0:T(8,128)(2,1)}, bf16[320,1024]{1,0:T(8,128)(2,1)}, bf16[320,1024]{1,0:T(8,128)(2,1)}, bf16[320,1024]{1,0:T(8,128)(2,1)}, bf16[3...) custom-call(bf16[320,3072]{1,0:T(8,128)(2,1)} %copy-done.1, bf16[320,3072]{1,0:T(8,128)(2,1)} %copy-done.11, ...), custom_call_target="tpu_custom_call" | custom-call | flops 8053063680 | tf_op jit(solution)/shard_map/forward/pallas_call | solution.py:289
  75.3 1.6 collective-permute-done.12.refs_3_
  76.9 2.3 %pack.3.grad.g_mine = bf16[320,3072]{1,0:T(8,128)(2,1)} custom-call(s32[4]{0:T(128)S(1)} %broadcast_multiply_fusion.starts, bf16[4,320,128]{2,1,0:T(8,128)(2,1)S(1)} %get-tuple-element.54.select, f32[4,320,128]{2,1,0:T(8,128)S(1)} %get-tuple-element.55.route_rows, bf16[128,3072]{1,0:T(8,128)(2,1)S(1)} %copy-done.14, ...), custom_call_target="tpu_custom_call" | custom-call | tf_op jit(solution)/shard_map/pack/pallas_call | solution.py:267
  79.2 2.8 %copy-done = bf16[1,1024,3072]{2,1,0:T(8,128)(2,1)S(1)} copy-done((bf16[1,1024,3072]{2,1,0:T(8,128)(2,1)S(1)}, bf16[1,1024,3072]{2,1,0:T(8,128)(2,1)}, u32[]{:S(2)}) %copy-start) | copy-done | bytes 6291480
  82.0 1.1 copy-done.20
  83.1 4.9 %backward.2 = (bf16[640,1024]{1,0:T(8,128)(2,1)S(1)}, bf16[640,1024]{1,0:T(8,128)(2,1)S(1)}) custom-call(bf16[320,3072]{1,0:T(8,128)(2,1)} %pack.3.grad.g_mine, bf16[1,1024,3072]{2,1,0:T(8,128)(2,1)S(1)} %copy-done, bf16[320,1024]{1,0:T(8,128)(2,1)S(1)} %copy-done.19, bf16[320,1024]{1,0:T(8,128)(2,1)S(1)} %copy-done.20), custom_call_target="tpu_custom_call" | custom-call | tf_op jit(solution)/shard_map/backward/pallas_call | solution.py:306
  88.1 4.9 %backward.3 = (bf16[640,1024]{1,0:T(8,128)(2,1)S(1)}, bf16[640,1024]{1,0:T(8,128)(2,1)S(1)}) custom-call(bf16[320,3072]{1,0:T(8,128)(2,1)} %collective-permute-done.13.grad.g_other, bf16[1,1024,3072]{2,1,0:T(8,128)(2,1)S(1)} %bitcast.26, bf16[320,1024]{1,0:T(8,128)(2,1)S(1)} %copy-done.17, ...), custom_call_target="tpu_custom_call", output_to_operand_aliasing={{0}: (4, {}), {1}: (5, {})} | custom-call | tf_op jit(solution)/shard_map/backward/pallas_call | solution.py:306
  93.1 2.2 %fusion.3 = f32[640,1536]{1,0:T(8,128)S(1)} fusion(bf16[640,1024]{1,0:T(8,128)(2,1)S(1)} %get-tuple-element.75.d_up, bf16[1,3072,1024]{2,1,0:T(8,128)(2,1)S(1)} %bitcast.28), kind=kOutput, calls=%fused_computation.5 | convolution fusion | flops 2013265920 | bytes 8388608 | tf_op jit(solution)/shard_map/dot_general | solution.py:20
  95.6 2.2 %add_convert_fusion.1.part = bf16[640,1536]{1,0:T(8,128)(2,1)S(1)} fusion(f32[640,1536]{1,0:T(8,128)S(1)} %fusion.3, bf16[640,1024]{1,0:T(8,128)(2,1)S(1)} %get-tuple-element.74.d_gate, bf16[1,3072,1024]{2,1,0:T(8,128)(2,1)S(1)} %bitcast.30), kind=kOutput, calls=%fused_computation.1 | convolution fusion | flops 2015232000 | bytes 10354688 | tf_op jit(solution)/shard_map/dot_general | solution.py:20
  98.5 2.2 %fusion = f32[640,1536]{1,0:T(8,128)S(1)} fusion(bf16[640,1024]{1,0:T(8,128)(2,1)S(1)} %get-tuple-element.75.d_up, bf16[1,3072,1024]{2,1,0:T(8,128)(2,1)S(1)} %bitcast.28), kind=kOutput, calls=%fused_computation.2 | convolution fusion | flops 2013265920 | bytes 8388608 | tf_op jit(solution)/shard_map/dot_general | solution.py:20
  100.7 2.2 %add_convert_fusion.part = bf16[640,1536]{1,0:T(8,128)(2,1)S(1)} fusion(f32[640,1536]{1,0:T(8,128)S(1)} %fusion, bf16[640,1024]{1,0:T(8,128)(2,1)S(1)} %get-tuple-element.74.d_gate, bf16[1,3072,1024]{2,1,0:T(8,128)(2,1)S(1)} %bitcast.30), kind=kOutput, calls=%fused_computation | convolution fusion | flops 2015232000 | bytes 10354688 | tf_op jit(solution)/shard_map/dot_general | solution.py:20
  103.1 1.4 merge.2
  105.3 1.5 collective-permute-start.16
  106.8 1.3 collective-permute-start.17
  108.1 1.5 merge.3
  110.3 1.5 collective-permute-start.26
  111.8 1.5 collective-permute-done.15.refs_1_
  114.0 1.7 %collective-permute-start.27 = (bf16[320,384]{1,0:T(8,128)(2,1)}, bf16[320,384]{1,0:T(8,128)(2,1)S(1)}, u32[]{:S(2)}, u32[]{:S(2)}) collective-permute-start(bf16[320,384]{1,0:T(8,128)(2,1)} %get-tuple-element.97), channel_id=1, source_target_pairs={{0,24},{8,16},{16,8},{24,0},{1,25},{9,17},{17,9},{25,1},{2,26},{10... | collective-permute-start | bytes 737288 | tf_op jit(solution)/shard_map/ppermute | solution.py:32
  116.1 1.9 %copy-done.7 = bf16[512,3072]{1,0:T(8,128)(2,1)S(1)} copy-done((bf16[512,3072]{1,0:T(8,128)(2,1)S(1)}, bf16[512,3072]{1,0:T(8,128)(2,1)}, u32[]{:S(2)}) %copy-start.7) | copy-done | bytes 3145752
  118.0 1.5 copy-done.12
  119.6 7.2 %low.1 = (bf16[320,512]{1,0:T(8,128)(2,1)S(1)}, bf16[320,512]{1,0:T(8,128)(2,1)S(1)}, bf16[320,512]{1,0:T(8,128)(2,1)S(1)}, bf16[320,512]{1,0:T(8,128)(2,1)S(1)}) custom-call(bf16[320,3072]{1,0:T(8,128)(2,1)S(1)} %copy-done.2, bf16[320,3072]{1,0:T(8,128)(2,1)S(1)} %copy-done.12, bf16[320,3072]{1,0:T(8,128)(2,1)} %pack.3.grad.g_mine, ...), custom_call_target="tpu_custom_call" | custom-call | tf_op jit(solution)/shard_map/low/pallas_call | solution.py:361
  126.9 1.5 to_tokens.2
  128.4 1.1 collective-permute-start.18
  130.4 2.5 %collective-permute-start.20 = (bf16[128,384]{1,0:T(8,128)(2,1)S(1)}, bf16[128,384]{1,0:T(8,128)(2,1)S(1)}, u32[]{:S(2)}, u32[]{:S(2)}) collective-permute-start(bf16[128,384]{1,0:T(8,128)(2,1)S(1)} %get-tuple-element.89), channel_id=1, source_target_pairs={{0,6},{1,7},{2,4},{3,5},{4,2},{5,3},{6,0},{7,1},{8,14},{9,15},{10,... | collective-permute-start | bytes 294920 | tf_op jit(solution)/shard_map/ppermute | solution.py:44
  132.9 6.0 %momentum.1 = (f32[1,512,1024]{2,1,0:T(8,128)}, f32[1,512,1024]{2,1,0:T(8,128)}, f32[1,1024,512]{2,1,0:T(8,128)}) custom-call(bf16[320,512]{1,0:T(8,128)(2,1)S(1)} %get-tuple-element.78.lt0, bf16[320,512]{1,0:T(8,128)(2,1)S(1)} %get-tuple-element.79.lt1, bf16[320,512]{1,0:T(8,128)(2,1)S(1)} %get-tuple-element.80.lg0, ...), custom_call_target="tpu_custom_call" | custom-call | tf_op jit(solution)/shard_map/momentum/pallas_call | solution.py:374
  139.6 1.8 %collective-permute-start.29 = (bf16[128,384]{1,0:T(8,128)(2,1)S(1)}, bf16[128,384]{1,0:T(8,128)(2,1)S(1)}, u32[]{:S(2)}, u32[]{:S(2)}) collective-permute-start(bf16[128,384]{1,0:T(8,128)(2,1)S(1)} %get-tuple-element.100), channel_id=1, source_target_pairs={{0,4},{1,5},{2,6},{3,7},{4,0},{5,1},{6,2},{7,3},{8,12},{9,13},{10,... | collective-permute-start | bytes 294920 | tf_op jit(solution)/shard_map/ppermute | solution.py:44
  141.5 2.5 %collective-permute-start.30 = (bf16[128,384]{1,0:T(8,128)(2,1)S(1)}, bf16[128,384]{1,0:T(8,128)(2,1)S(1)}, u32[]{:S(2)}, u32[]{:S(2)}) collective-permute-start(bf16[128,384]{1,0:T(8,128)(2,1)S(1)} %get-tuple-element.101), channel_id=1, source_target_pairs={{0,6},{1,7},{2,4},{3,5},{4,2},{5,3},{6,0},{7,1},{8,14},{9,15},{10,... | collective-permute-start | bytes 294920 | tf_op jit(solution)/shard_map/ppermute | solution.py:44
  144.0 2.5 %collective-permute-start.23 = (bf16[128,384]{1,0:T(8,128)(2,1)S(1)}, bf16[128,384]{1,0:T(8,128)(2,1)S(1)}, u32[]{:S(2)}, u32[]{:S(2)}) collective-permute-start(bf16[128,384]{1,0:T(8,128)(2,1)S(1)} %add_convert_fusion.3.refs_0_), channel_id=1, source_target_pairs={{0,24},{8,16},{16,8},{24,0},{1,25},{9,17},{17,9},{25,1},{2,26},{10... | collective-permute-start | bytes 294920 | tf_op jit(solution)/shard_map/ppermute | solution.py:32
  147.5 2.3 %collective-permute-done.29 = bf16[128,384]{1,0:T(8,128)(2,1)S(1)} collective-permute-done((bf16[128,384]{1,0:T(8,128)(2,1)S(1)}, bf16[128,384]{1,0:T(8,128)(2,1)S(1)}, u32[]{:S(2)}, u32[]{:S(2)}) %collective-permute-start.29) | collective-permute-done | bytes 98336 | tf_op jit(solution)/shard_map/ppermute | solution.py:44
  149.9 2.6 %collective-permute-start.33 = (bf16[128,384]{1,0:T(8,128)(2,1)S(1)}, bf16[128,384]{1,0:T(8,128)(2,1)S(1)}, u32[]{:S(2)}, u32[]{:S(2)}) collective-permute-start(bf16[128,384]{1,0:T(8,128)(2,1)S(1)} %add_convert_fusion.2.refs_4_), channel_id=1, source_target_pairs={{0,24},{8,16},{16,8},{24,0},{1,25},{9,17},{17,9},{25,1},{2,26},{10... | collective-permute-start | bytes 294920 | tf_op jit(solution)/shard_map/ppermute | solution.py:32
  153.5 2.0 %collective-permute-done.33.refs_7_ = bf16[128,384]{1,0:T(8,128)(2,1)S(1)} collective-permute-done((bf16[128,384]{1,0:T(8,128)(2,1)S(1)}, bf16[128,384]{1,0:T(8,128)(2,1)S(1)}, u32[]{:S(2)}, u32[]{:S(2)}) %collective-permute-start.33) | collective-permute-done | bytes 98336 | tf_op jit(solution)/shard_map/ppermute | solution.py:32
  155.5 1.6 collective-permute-done.32.refs_6_
  157.7 1.5 place.1
  (119 shorter events, 14.5 us)
Async XLA Ops:
  7.2 48.8 %copy-start.13 = (bf16[128,3072]{1,0:T(8,128)(2,1)S(1)}, bf16[128,3072]{1,0:T(8,128)(2,1)}, u32[]{:S(2)}) copy-start(bf16[128,3072]{1,0:T(8,128)(2,1)} %whole.2) | copy-start | bytes 2359300
  7.2 109.0 %all-gather.2.cloned.1.call-start = ((), (), s32[]{:S(2)}) async-start(), calls=%async_computation | async-start | bytes 3538944 | tf_op jit(solution)/shard_map/all_gather | solution.py:358
  9.6 11.5 %collective-permute-start.2 = (bf16[144,768]{1,0:T(8,128)(2,1)S(1)}, bf16[144,768]{1,0:T(8,128)(2,1)S(1)}, u32[]{:S(2)}, u32[]{:S(2)}) collective-permute-start(bf16[144,768]{1,0:T(8,128)(2,1)S(1)} %fusion.11), channel_id=1, source_target_pairs={{0,6},{1,7},{2,4},{3,5},{4,2},{5,3},{6,0},{7,1},{8,14},{9,15},{10,... | collective-permute-start | bytes 663560 | tf_op jit(solution)/shard_map/ppermute | solution.py:44
  14.8 18.8 %collective-permute-start.1 = (bf16[144,768]{1,0:T(8,128)(2,1)S(1)}, bf16[144,768]{1,0:T(8,128)(2,1)S(1)}, u32[]{:S(2)}, u32[]{:S(2)}) collective-permute-start(bf16[144,768]{1,0:T(8,128)(2,1)S(1)} %fusion.11), channel_id=1, source_target_pairs={{0,4},{1,5},{2,6},{3,7},{4,0},{5,1},{6,2},{7,3},{8,12},{9,13},{10,... | collective-permute-start | bytes 663560 | tf_op jit(solution)/shard_map/ppermute | solution.py:44
  14.8 18.8 %collective-permute-start = (bf16[144,768]{1,0:T(8,128)(2,1)S(1)}, bf16[144,768]{1,0:T(8,128)(2,1)S(1)}, u32[]{:S(2)}, u32[]{:S(2)}) collective-permute-start(bf16[144,768]{1,0:T(8,128)(2,1)S(1)} %fusion.11), channel_id=1, source_target_pairs={{0,2},{1,3},{2,0},{3,1},{4,6},{5,7},{6,4},{7,5},{8,10},{9,11},{10,... | collective-permute-start | bytes 663560 | tf_op jit(solution)/shard_map/ppermute | solution.py:44
  33.6 7.9 %collective-permute-start.5 = (bf16[128,768]{1,0:T(8,128)(2,1)S(1)}, bf16[128,768]{1,0:T(8,128)(2,1)S(1)}, u32[]{:S(2)}, u32[]{:S(2)}) collective-permute-start(bf16[128,768]{1,0:T(8,128)(2,1)S(1)} %constant_dynamic-slice_fusion), channel_id=1, source_target_pairs={{0,6},{1,7},{2,4},{3,5},{4,2},{5,3},{6,0},{7,1},{8,14},{9,15},{10,... | collective-permute-start | bytes 589832 | tf_op jit(solution)/shard_map/ppermute | solution.py:44
  37.8 16.1 %collective-permute-start.6 = (bf16[240,768]{1,0:T(8,128)(2,1)S(1)}, bf16[240,768]{1,0:T(8,128)(2,1)S(1)}, u32[]{:S(2)}, u32[]{:S(2)}) collective-permute-start(bf16[240,768]{1,0:T(8,128)(2,1)S(1)} %get-tuple-element.60), channel_id=1, source_target_pairs={{0,8},{8,0},{16,24},{24,16},{1,9},{9,1},{17,25},{25,17},{2,10},{10... | collective-permute-start | bytes 1105928 | tf_op jit(solution)/shard_map/ppermute | solution.py:32
  39.3 16.6 %collective-permute-start.7 = (bf16[240,768]{1,0:T(8,128)(2,1)S(1)}, bf16[240,768]{1,0:T(8,128)(2,1)S(1)}, u32[]{:S(2)}, u32[]{:S(2)}) collective-permute-start(bf16[240,768]{1,0:T(8,128)(2,1)S(1)} %get-tuple-element.61), channel_id=1, source_target_pairs={{0,16},{8,24},{16,0},{24,8},{1,17},{9,25},{17,1},{25,9},{2,18},{10... | collective-permute-start | bytes 1105928 | tf_op jit(solution)/shard_map/ppermute | solution.py:32
  40.9 15.1 %collective-permute-start.8 = (bf16[240,768]{1,0:T(8,128)(2,1)S(1)}, bf16[240,768]{1,0:T(8,128)(2,1)S(1)}, u32[]{:S(2)}, u32[]{:S(2)}) collective-permute-start(bf16[240,768]{1,0:T(8,128)(2,1)S(1)} %get-tuple-element.62), channel_id=1, source_target_pairs={{0,24},{8,16},{16,8},{24,0},{1,25},{9,17},{17,9},{25,1},{2,26},{10... | collective-permute-start | bytes 1105928 | tf_op jit(solution)/shard_map/ppermute | solution.py:32
  41.3 9.9 %collective-permute-start.4 = (bf16[128,768]{1,0:T(8,128)(2,1)S(1)}, bf16[128,768]{1,0:T(8,128)(2,1)S(1)}, u32[]{:S(2)}, u32[]{:S(2)}) collective-permute-start(bf16[128,768]{1,0:T(8,128)(2,1)S(1)} %constant_dynamic-slice_fusion), channel_id=1, source_target_pairs={{0,4},{1,5},{2,6},{3,7},{4,0},{5,1},{6,2},{7,3},{8,12},{9,13},{10,... | collective-permute-start | bytes 589832 | tf_op jit(solution)/shard_map/ppermute | solution.py:44
  41.4 11.9 %collective-permute-start.3 = (bf16[128,768]{1,0:T(8,128)(2,1)S(1)}, bf16[128,768]{1,0:T(8,128)(2,1)S(1)}, u32[]{:S(2)}, u32[]{:S(2)}) collective-permute-start(bf16[128,768]{1,0:T(8,128)(2,1)S(1)} %constant_dynamic-slice_fusion), channel_id=1, source_target_pairs={{0,2},{1,3},{2,0},{3,1},{4,6},{5,7},{6,4},{7,5},{8,10},{9,11},{10,... | collective-permute-start | bytes 589832 | tf_op jit(solution)/shard_map/ppermute | solution.py:44
  56.9 4.0 %collective-permute-start.9 = (bf16[320,3072]{1,0:T(8,128)(2,1)S(1)}, bf16[320,3072]{1,0:T(8,128)(2,1)S(1)}, u32[]{:S(2)}, u32[]{:S(2)}) collective-permute-start(bf16[320,3072]{1,0:T(8,128)(2,1)S(1)} %pack.2.mine), channel_id=1, source_target_pairs={{0,1},{1,0},{2,3},{3,2},{4,5},{5,4},{6,7},{7,6},{8,9},{9,8},{10,11... | collective-permute-start | bytes 5898248 | tf_op jit(solution)/shard_map/ppermute | solution.py:36
  57.0 18.3 %collective-permute-start.10 = (bf16[240,768]{1,0:T(8,128)(2,1)S(1)}, bf16[240,768]{1,0:T(8,128)(2,1)S(1)}, u32[]{:S(2)}, u32[]{:S(2)}) collective-permute-start(bf16[240,768]{1,0:T(8,128)(2,1)S(1)} %get-tuple-element.65), channel_id=1, source_target_pairs={{0,8},{8,0},{16,24},{24,16},{1,9},{9,1},{17,25},{25,17},{2,10},{10... | collective-permute-start | bytes 1105928 | tf_op jit(solution)/shard_map/ppermute | solution.py:32
  58.3 17.0 %collective-permute-start.11 = (bf16[240,768]{1,0:T(8,128)(2,1)S(1)}, bf16[240,768]{1,0:T(8,128)(2,1)S(1)}, u32[]{:S(2)}, u32[]{:S(2)}) collective-permute-start(bf16[240,768]{1,0:T(8,128)(2,1)S(1)} %get-tuple-element.66), channel_id=1, source_target_pairs={{0,16},{8,24},{16,0},{24,8},{1,17},{9,25},{17,1},{25,9},{2,18},{10... | collective-permute-start | bytes 1105928 | tf_op jit(solution)/shard_map/ppermute | solution.py:32
  59.1 17.7 %copy-start.14 = (bf16[128,3072]{1,0:T(8,128)(2,1)S(1)}, bf16[128,3072]{1,0:T(8,128)(2,1)}, u32[]{:S(2)}) copy-start(bf16[128,3072]{1,0:T(8,128)(2,1)} %whole.3) | copy-start | bytes 2359300
  59.1 17.7 %collective-permute-start.12 = (bf16[240,768]{1,0:T(8,128)(2,1)S(1)}, bf16[240,768]{1,0:T(8,128)(2,1)S(1)}, u32[]{:S(2)}, u32[]{:S(2)}) collective-permute-start(bf16[240,768]{1,0:T(8,128)(2,1)S(1)} %get-tuple-element.67), channel_id=1, source_target_pairs={{0,24},{8,16},{16,8},{24,0},{1,25},{9,17},{17,9},{25,1},{2,26},{10... | collective-permute-start | bytes 1105928 | tf_op jit(solution)/shard_map/ppermute | solution.py:32
  76.9 11.2 %slice-start = ((s8[6291456]{0:T(1024)(128)(4,1)}), s8[2097152]{0:T(1024)(128)(4,1)S(1)}, s32[]{:S(2)}) async-start(s8[6291456]{0:T(1024)(128)(4,1)} %bitcast.25), calls=%async_computation.1 | async-start | bytes 4194304
  79.2 8.9 %collective-permute-start.13 = (bf16[320,3072]{1,0:T(8,128)(2,1)}, bf16[320,3072]{1,0:T(8,128)(2,1)}, u32[]{:S(2)}, u32[]{:S(2)}) collective-permute-start(bf16[320,3072]{1,0:T(8,128)(2,1)} %pack.3.grad.g_mine), channel_id=1, source_target_pairs={{0,1},{1,0},{2,3},{3,2},{4,5},{5,4},{6,7},{7,6},{8,9},{9,8},{10,11... | collective-permute-start | bytes 5898248 | tf_op jit(solution)/shard_map/ppermute | solution.py:36
  83.1 9.9 %slice-start.2 = ((s8[6291456]{0:T(1024)(128)(4,1)}), s8[4194304]{0:T(1024)(128)(4,1)S(1)}, s32[]{:S(2)}) async-start(s8[6291456]{0:T(1024)(128)(4,1)} %bitcast.27), calls=%async_computation.3 | async-start | bytes 8388608
  97.9 5.2 %collective-permute-start.14 = (bf16[320,1536]{1,0:T(8,128)(2,1)S(1)}, bf16[320,1536]{1,0:T(8,128)(2,1)S(1)}, u32[]{:S(2)}, u32[]{:S(2)}) collective-permute-start(bf16[320,1536]{1,0:T(8,128)(2,1)S(1)} %slice.24), channel_id=1, source_target_pairs={{0,1},{1,0},{2,3},{3,2},{4,5},{5,4},{6,7},{7,6},{8,9},{9,8},{10,11... | collective-permute-start | bytes 2949128 | tf_op jit(solution)/shard_map/ppermute | solution.py:36
  103.0 13.1 %copy-start.2 = (bf16[320,3072]{1,0:T(8,128)(2,1)S(1)}, bf16[320,3072]{1,0:T(8,128)(2,1)}, u32[]{:S(2)}) copy-start(bf16[320,3072]{1,0:T(8,128)(2,1)} %copy-done.1) | copy-start | bytes 5898244
  103.0 5.0 %collective-permute-start.24 = (bf16[320,1536]{1,0:T(8,128)(2,1)S(1)}, bf16[320,1536]{1,0:T(8,128)(2,1)S(1)}, u32[]{:S(2)}, u32[]{:S(2)}) collective-permute-start(bf16[320,1536]{1,0:T(8,128)(2,1)S(1)} %slice.25), channel_id=1, source_target_pairs={{0,1},{1,0},{2,3},{3,2},{4,5},{5,4},{6,7},{7,6},{8,9},{9,8},{10,11... | collective-permute-start | bytes 2949128 | tf_op jit(solution)/shard_map/ppermute | solution.py:36
  104.6 8.8 %copy-start.21 = (bf16[320,384]{1,0:T(8,128)(2,1)}, bf16[320,384]{1,0:T(8,128)(2,1)S(1)}, u32[]{:S(2)}) copy-start(bf16[320,384]{1,0:T(8,128)(2,1)S(1)} %get-tuple-element.82.refs_0_) | copy-start | bytes 737284
  104.6 8.8 %collective-permute-start.15 = (bf16[320,384]{1,0:T(8,128)(2,1)S(1)}, bf16[320,384]{1,0:T(8,128)(2,1)S(1)}, u32[]{:S(2)}, u32[]{:S(2)}) collective-permute-start(bf16[320,384]{1,0:T(8,128)(2,1)S(1)} %get-tuple-element.83), channel_id=1, source_target_pairs={{0,8},{8,0},{16,24},{24,16},{1,9},{9,1},{17,25},{25,17},{2,10},{10... | collective-permute-start | bytes 737288 | tf_op jit(solution)/shard_map/ppermute | solution.py:32
  105.3 21.6 %collective-permute-start.16 = (bf16[320,384]{1,0:T(8,128)(2,1)}, bf16[320,384]{1,0:T(8,128)(2,1)}, u32[]{:S(2)}, u32[]{:S(2)}) collective-permute-start(bf16[320,384]{1,0:T(8,128)(2,1)} %get-tuple-element.84), channel_id=1, source_target_pairs={{0,16},{8,24},{16,0},{24,8},{1,17},{9,25},{17,1},{25,9},{2,18},{10... | collective-permute-start | bytes 737288 | tf_op jit(solution)/shard_map/ppermute | solution.py:32
  106.8 20.1 %collective-permute-start.17 = (bf16[320,384]{1,0:T(8,128)(2,1)}, bf16[320,384]{1,0:T(8,128)(2,1)}, u32[]{:S(2)}, u32[]{:S(2)}) collective-permute-start(bf16[320,384]{1,0:T(8,128)(2,1)} %get-tuple-element.85), channel_id=1, source_target_pairs={{0,24},{8,16},{16,8},{24,0},{1,25},{9,17},{17,9},{25,1},{2,26},{10... | collective-permute-start | bytes 737288 | tf_op jit(solution)/shard_map/ppermute | solution.py:32
  109.6 20.8 %collective-permute-start.25 = (bf16[320,384]{1,0:T(8,128)(2,1)}, bf16[320,384]{1,0:T(8,128)(2,1)S(1)}, u32[]{:S(2)}, u32[]{:S(2)}) collective-permute-start(bf16[320,384]{1,0:T(8,128)(2,1)} %get-tuple-element.95), channel_id=1, source_target_pairs={{0,8},{8,0},{16,24},{24,16},{1,9},{9,1},{17,25},{25,17},{2,10},{10... | collective-permute-start | bytes 737288 | tf_op jit(solution)/shard_map/ppermute | solution.py:32
  110.3 28.6 %collective-permute-start.26 = (bf16[320,384]{1,0:T(8,128)(2,1)}, bf16[320,384]{1,0:T(8,128)(2,1)S(1)}, u32[]{:S(2)}, u32[]{:S(2)}) collective-permute-start(bf16[320,384]{1,0:T(8,128)(2,1)} %get-tuple-element.96), channel_id=1, source_target_pairs={{0,16},{8,24},{16,0},{24,8},{1,17},{9,25},{17,1},{25,9},{2,18},{10... | collective-permute-start | bytes 737288 | tf_op jit(solution)/shard_map/ppermute | solution.py:32
  114.0 25.0 %collective-permute-start.27 = (bf16[320,384]{1,0:T(8,128)(2,1)}, bf16[320,384]{1,0:T(8,128)(2,1)S(1)}, u32[]{:S(2)}, u32[]{:S(2)}) collective-permute-start(bf16[320,384]{1,0:T(8,128)(2,1)} %get-tuple-element.97), channel_id=1, source_target_pairs={{0,24},{8,16},{16,8},{24,0},{1,25},{9,17},{17,9},{25,1},{2,26},{10... | collective-permute-start | bytes 737288 | tf_op jit(solution)/shard_map/ppermute | solution.py:32
  119.6 13.3 %copy-start.4 = (bf16[640,1024]{1,0:T(8,128)(2,1)S(1)}, bf16[640,1024]{1,0:T(8,128)(2,1)}, u32[]{:S(2)}) copy-start(bf16[640,1024]{1,0:T(8,128)(2,1)} %copy-done.3) | copy-start | bytes 3932164
  119.6 13.3 %copy-start.6 = (bf16[640,1024]{1,0:T(8,128)(2,1)S(1)}, bf16[640,1024]{1,0:T(8,128)(2,1)}, u32[]{:S(2)}) copy-start(bf16[640,1024]{1,0:T(8,128)(2,1)} %copy-done.5) | copy-start | bytes 3932164
  119.6 13.3 %copy-start.8 = (f32[1,512,1024]{2,1,0:T(8,128)S(1)}, f32[1,512,1024]{2,1,0:T(8,128)}, u32[]{:S(2)}) copy-start(f32[1,512,1024]{2,1,0:T(8,128)} %mg.1) | copy-start | bytes 6291460
  119.6 13.3 %copy-start.9 = (f32[1,512,1024]{2,1,0:T(8,128)S(1)}, f32[1,512,1024]{2,1,0:T(8,128)}, u32[]{:S(2)}) copy-start(f32[1,512,1024]{2,1,0:T(8,128)} %mu.1) | copy-start | bytes 6291460
  119.6 13.3 %copy-start.10 = (f32[1,1024,512]{2,1,0:T(8,128)S(1)}, f32[1,1024,512]{2,1,0:T(8,128)}, u32[]{:S(2)}) copy-start(f32[1,1024,512]{2,1,0:T(8,128)} %md.1) | copy-start | bytes 6291460
  119.6 13.3 %copy-start.15 = (bf16[320,1024]{1,0:T(8,128)(2,1)S(1)}, bf16[320,1024]{1,0:T(8,128)(2,1)}, u32[]{:S(2)}) copy-start(bf16[320,1024]{1,0:T(8,128)(2,1)} %get-tuple-element.63.h0) | copy-start | bytes 1966084
  119.6 13.3 %copy-start.16 = (bf16[320,1024]{1,0:T(8,128)(2,1)S(1)}, bf16[320,1024]{1,0:T(8,128)(2,1)}, u32[]{:S(2)}) copy-start(bf16[320,1024]{1,0:T(8,128)(2,1)} %get-tuple-element.92.h1) | copy-start | bytes 1966084
  128.4 13.0 %collective-permute-start.18 = (bf16[128,384]{1,0:T(8,128)(2,1)S(1)}, bf16[128,384]{1,0:T(8,128)(2,1)S(1)}, u32[]{:S(2)}, u32[]{:S(2)}) collective-permute-start(bf16[128,384]{1,0:T(8,128)(2,1)S(1)} %get-tuple-element.87), channel_id=1, source_target_pairs={{0,2},{1,3},{2,0},{3,1},{4,6},{5,7},{6,4},{7,5},{8,10},{9,11},{10,... | collective-permute-start | bytes 294920 | tf_op jit(solution)/shard_map/ppermute | solution.py:44
  129.5 14.4 %collective-permute-start.19 = (bf16[128,384]{1,0:T(8,128)(2,1)S(1)}, bf16[128,384]{1,0:T(8,128)(2,1)S(1)}, u32[]{:S(2)}, u32[]{:S(2)}) collective-permute-start(bf16[128,384]{1,0:T(8,128)(2,1)S(1)} %get-tuple-element.88), channel_id=1, source_target_pairs={{0,4},{1,5},{2,6},{3,7},{4,0},{5,1},{6,2},{7,3},{8,12},{9,13},{10,... | collective-permute-start | bytes 294920 | tf_op jit(solution)/shard_map/ppermute | solution.py:44
  130.4 13.5 %collective-permute-start.20 = (bf16[128,384]{1,0:T(8,128)(2,1)S(1)}, bf16[128,384]{1,0:T(8,128)(2,1)S(1)}, u32[]{:S(2)}, u32[]{:S(2)}) collective-permute-start(bf16[128,384]{1,0:T(8,128)(2,1)S(1)} %get-tuple-element.89), channel_id=1, source_target_pairs={{0,6},{1,7},{2,4},{3,5},{4,2},{5,3},{6,0},{7,1},{8,14},{9,15},{10,... | collective-permute-start | bytes 294920 | tf_op jit(solution)/shard_map/ppermute | solution.py:44
  139.5 7.6 %collective-permute-start.28 = (bf16[128,384]{1,0:T(8,128)(2,1)S(1)}, bf16[128,384]{1,0:T(8,128)(2,1)S(1)}, u32[]{:S(2)}, u32[]{:S(2)}) collective-permute-start(bf16[128,384]{1,0:T(8,128)(2,1)S(1)} %get-tuple-element.99), channel_id=1, source_target_pairs={{0,2},{1,3},{2,0},{3,1},{4,6},{5,7},{6,4},{7,5},{8,10},{9,11},{10,... | collective-permute-start | bytes 294920 | tf_op jit(solution)/shard_map/ppermute | solution.py:44
  139.6 10.2 %collective-permute-start.29 = (bf16[128,384]{1,0:T(8,128)(2,1)S(1)}, bf16[128,384]{1,0:T(8,128)(2,1)S(1)}, u32[]{:S(2)}, u32[]{:S(2)}) collective-permute-start(bf16[128,384]{1,0:T(8,128)(2,1)S(1)} %get-tuple-element.100), channel_id=1, source_target_pairs={{0,4},{1,5},{2,6},{3,7},{4,0},{5,1},{6,2},{7,3},{8,12},{9,13},{10,... | collective-permute-start | bytes 294920 | tf_op jit(solution)/shard_map/ppermute | solution.py:44
  141.5 8.4 %collective-permute-start.30 = (bf16[128,384]{1,0:T(8,128)(2,1)S(1)}, bf16[128,384]{1,0:T(8,128)(2,1)S(1)}, u32[]{:S(2)}, u32[]{:S(2)}) collective-permute-start(bf16[128,384]{1,0:T(8,128)(2,1)S(1)} %get-tuple-element.101), channel_id=1, source_target_pairs={{0,6},{1,7},{2,4},{3,5},{4,2},{5,3},{6,0},{7,1},{8,14},{9,15},{10,... | collective-permute-start | bytes 294920 | tf_op jit(solution)/shard_map/ppermute | solution.py:44
  144.0 9.1 %collective-permute-start.23 = (bf16[128,384]{1,0:T(8,128)(2,1)S(1)}, bf16[128,384]{1,0:T(8,128)(2,1)S(1)}, u32[]{:S(2)}, u32[]{:S(2)}) collective-permute-start(bf16[128,384]{1,0:T(8,128)(2,1)S(1)} %add_convert_fusion.3.refs_0_), channel_id=1, source_target_pairs={{0,24},{8,16},{16,8},{24,0},{1,25},{9,17},{17,9},{25,1},{2,26},{10... | collective-permute-start | bytes 294920 | tf_op jit(solution)/shard_map/ppermute | solution.py:32
  146.5 7.0 %collective-permute-start.22 = (bf16[128,384]{1,0:T(8,128)(2,1)S(1)}, bf16[128,384]{1,0:T(8,128)(2,1)S(1)}, u32[]{:S(2)}, u32[]{:S(2)}) collective-permute-start(bf16[128,384]{1,0:T(8,128)(2,1)S(1)} %add_convert_fusion.3.refs_0_), channel_id=1, source_target_pairs={{0,16},{8,24},{16,0},{24,8},{1,17},{9,25},{17,1},{25,9},{2,18},{10... | collective-permute-start | bytes 294920 | tf_op jit(solution)/shard_map/ppermute | solution.py:32
  147.1 6.4 %collective-permute-start.21 = (bf16[128,384]{1,0:T(8,128)(2,1)S(1)}, bf16[128,384]{1,0:T(8,128)(2,1)S(1)}, u32[]{:S(2)}, u32[]{:S(2)}) collective-permute-start(bf16[128,384]{1,0:T(8,128)(2,1)S(1)} %add_convert_fusion.3.refs_0_), channel_id=1, source_target_pairs={{0,8},{8,0},{16,24},{24,16},{1,9},{9,1},{17,25},{25,17},{2,10},{10... | collective-permute-start | bytes 294920 | tf_op jit(solution)/shard_map/ppermute | solution.py:32
  149.9 5.6 %collective-permute-start.33 = (bf16[128,384]{1,0:T(8,128)(2,1)S(1)}, bf16[128,384]{1,0:T(8,128)(2,1)S(1)}, u32[]{:S(2)}, u32[]{:S(2)}) collective-permute-start(bf16[128,384]{1,0:T(8,128)(2,1)S(1)} %add_convert_fusion.2.refs_4_), channel_id=1, source_target_pairs={{0,24},{8,16},{16,8},{24,0},{1,25},{9,17},{17,9},{25,1},{2,26},{10... | collective-permute-start | bytes 294920 | tf_op jit(solution)/shard_map/ppermute | solution.py:32
  152.5 4.6 %collective-permute-start.32 = (bf16[128,384]{1,0:T(8,128)(2,1)S(1)}, bf16[128,384]{1,0:T(8,128)(2,1)S(1)}, u32[]{:S(2)}, u32[]{:S(2)}) collective-permute-start(bf16[128,384]{1,0:T(8,128)(2,1)S(1)} %add_convert_fusion.2.refs_4_), channel_id=1, source_target_pairs={{0,16},{8,24},{16,0},{24,8},{1,17},{9,25},{17,1},{25,9},{2,18},{10... | collective-permute-start | bytes 294920 | tf_op jit(solution)/shard_map/ppermute | solution.py:32
  153.0 4.6 %collective-permute-start.31 = (bf16[128,384]{1,0:T(8,128)(2,1)S(1)}, bf16[128,384]{1,0:T(8,128)(2,1)S(1)}, u32[]{:S(2)}, u32[]{:S(2)}) collective-permute-start(bf16[128,384]{1,0:T(8,128)(2,1)S(1)} %add_convert_fusion.2.refs_4_), channel_id=1, source_target_pairs={{0,8},{8,0},{16,24},{24,16},{1,9},{9,1},{17,25},{25,17},{2,10},{10... | collective-permute-start | bytes 294920 | tf_op jit(solution)/shard_map/ppermute | solution.py:32
  (18 other events, 74.6 us)
Sparse Core Ops, SparseCore 0:
  79.3 36.7 all-gather.1

commit v3 on v2

--- a/solution.py
+++ b/solution.py
@@ -302,16 +302,18 @@
     grad_other = core_swap(grad_mine, count_fsdp)
 
     def backward(number, grad, silu, factor, *held):
-        rows = pl.BlockSpec((half, width_f), lambda i: (number, i))
+        width_b = tile_of(hidden_local, 512)
+        rows = pl.BlockSpec((half, width_b), lambda i: (number, i))
+        row_b = pl.BlockSpec((half, width_b), lambda i: (0, i))
         return call(
             back_kernel,
             "backward",
             [((2 * half, hidden_local), bf16)] * 2,
-            [vmem, pl.BlockSpec((1, width_f, width), lambda i: (0, i, 0)), row_f, row_f]
+            [vmem, pl.BlockSpec((1, width_b, width), lambda i: (0, i, 0)), row_b, row_b]
             + [pl.BlockSpec(memory_space=pl.ANY)] * len(held),
             [rows] * 2,
-            grid=(hidden_local // width_f,),
-        limit=14,
+            grid=(hidden_local // width_b,),
+        limit=20,
             alias={4: 0, 5: 1} if held else None,
         )(grad, w_down, silu, factor, *held)
 

time: 166 us -> 166 us (level)
  transfers between devices with their start and end apart: 35 -> 35, of which waited for: 14 -> 14; matrix products, arithmetic and copies ran while one was open for 6% -> 6% of each run, Pallas kernels for 26% -> 25%
where the time goes in v3:
time: 166 us
  starting transfers between devices  47.1 us (28%)
  Pallas kernels  46.8 us (28%)
  waiting for transfers between devices  35.1 us (21%)
  between operations  14.5 us (9%)
  local copies, waits for them, and re-layouts  11.7 us (7%)
  matrix products  8.92 us (5%)
    ppermute x12, starting transfers between devices, chip_swap(): lax.ppermute(array, 'fsdp', [(i, i ^ 2 * step) for i in range(count)])  24.7 us
    ppermute x12, waiting for transfers between devices, chip_swap(): lax.ppermute(array, 'fsdp', [(i, i ^ 2 * step) for i in range(count)])  24.1 us
    ppermute x18, starting transfers between devices, plane_swap(): return lax.ppermute(array, 'exp', [(i, i ^ step) for i in range(count)])  21.6 us
    pallas_call x1, Pallas kernels, shards(): call(forward_kernel, 'forward', [half_shape] * 6, [vmem, vmem, weight_f,...  13 us
    unnamed x62, local copies, waits for them, and re-layouts  9.65 us
    ppermute x18, waiting for transfers between devices, plane_swap(): return lax.ppermute(array, 'exp', [(i, i ^ step) for i in range(count)])  9.08 us
    pallas_call x2, Pallas kernels, backward(): call(back_kernel, 'backward', [((2 * half, hidden_local), bf16)] * 2, [vm...  9 us
    dot_general x4, matrix products, contract_last(): lax.dot_general(left, right, (((1,), (1,)), ((), ())), preferred_element_...  8.92 us
  transfers between devices with their start and end apart: 35, of which 14 were waited for; matrix products, arithmetic and copies ran while one was open for 6% of the time, Pallas kernels for 25%

profile of v3, /device:TPU:0, one launch (start us, length us, event | category | flops | bytes accessed | tf_op | source)
XLA Modules:
  0.0 165.7 jit_solution(11403861506383576636)
XLA Ops:
  9.6 5.1 %collective-permute-start.2 = (bf16[144,768]{1,0:T(8,128)(2,1)S(1)}, bf16[144,768]{1,0:T(8,128)(2,1)S(1)}, u32[]{:S(2)}, u32[]{:S(2)}) collective-permute-start(bf16[144,768]{1,0:T(8,128)(2,1)S(1)} %fusion.11), channel_id=1, source_target_pairs={{0,6},{1,7},{2,4},{3,5},{4,2},{5,3},{6,0},{7,1},{8,14},{9,15},{10,... | collective-permute-start | bytes 663560 | tf_op jit(solution)/shard_map/ppermute | solution.py:44
  16.3 4.8 %collective-permute-done.2.refs_2_ = bf16[144,768]{1,0:T(8,128)(2,1)S(1)} collective-permute-done((bf16[144,768]{1,0:T(8,128)(2,1)S(1)}, bf16[144,768]{1,0:T(8,128)(2,1)S(1)}, u32[]{:S(2)}, u32[]{:S(2)}) %collective-permute-start.2) | collective-permute-done | bytes 221216 | tf_op jit(solution)/shard_map/ppermute | solution.py:44
  21.2 12.4 %collective-permute-done.1.refs_1_ = bf16[144,768]{1,0:T(8,128)(2,1)S(1)} collective-permute-done((bf16[144,768]{1,0:T(8,128)(2,1)S(1)}, bf16[144,768]{1,0:T(8,128)(2,1)S(1)}, u32[]{:S(2)}, u32[]{:S(2)}) %collective-permute-start.1) | collective-permute-done | bytes 221216 | tf_op jit(solution)/shard_map/ppermute | solution.py:44
  33.6 2.7 %collective-permute-start.5 = (bf16[128,768]{1,0:T(8,128)(2,1)S(1)}, bf16[128,768]{1,0:T(8,128)(2,1)S(1)}, u32[]{:S(2)}, u32[]{:S(2)}) collective-permute-start(bf16[128,768]{1,0:T(8,128)(2,1)S(1)} %constant_dynamic-slice_fusion), channel_id=1, source_target_pairs={{0,6},{1,7},{2,4},{3,5},{4,2},{5,3},{6,0},{7,1},{8,14},{9,15},{10,... | collective-permute-start | bytes 589832 | tf_op jit(solution)/shard_map/ppermute | solution.py:44
  36.3 1.5 select.27
  37.8 1.6 collective-permute-start.6
  39.3 1.5 collective-permute-start.7
  41.4 7.4 %collective-permute-start.3 = (bf16[128,768]{1,0:T(8,128)(2,1)S(1)}, bf16[128,768]{1,0:T(8,128)(2,1)S(1)}, u32[]{:S(2)}, u32[]{:S(2)}) collective-permute-start(bf16[128,768]{1,0:T(8,128)(2,1)S(1)} %constant_dynamic-slice_fusion), channel_id=1, source_target_pairs={{0,2},{1,3},{2,0},{3,1},{4,6},{5,7},{6,4},{7,5},{8,10},{9,11},{10,... | collective-permute-start | bytes 589832 | tf_op jit(solution)/shard_map/ppermute | solution.py:44
  48.8 2.5 %collective-permute-done.4.refs_1_ = bf16[128,768]{1,0:T(8,128)(2,1)S(1)} collective-permute-done((bf16[128,768]{1,0:T(8,128)(2,1)S(1)}, bf16[128,768]{1,0:T(8,128)(2,1)S(1)}, u32[]{:S(2)}, u32[]{:S(2)}) %collective-permute-start.4) | collective-permute-done | bytes 196640 | tf_op jit(solution)/shard_map/ppermute | solution.py:44
  51.3 2.0 %collective-permute-done.3.refs_0_ = bf16[128,768]{1,0:T(8,128)(2,1)S(1)} collective-permute-done((bf16[128,768]{1,0:T(8,128)(2,1)S(1)}, bf16[128,768]{1,0:T(8,128)(2,1)S(1)}, u32[]{:S(2)}, u32[]{:S(2)}) %collective-permute-start.3) | collective-permute-done | bytes 196640 | tf_op jit(solution)/shard_map/ppermute | solution.py:44
  53.8 2.1 %collective-permute-done.7.refs_2_ = bf16[240,768]{1,0:T(8,128)(2,1)S(1)} collective-permute-done((bf16[240,768]{1,0:T(8,128)(2,1)S(1)}, bf16[240,768]{1,0:T(8,128)(2,1)S(1)}, u32[]{:S(2)}, u32[]{:S(2)}) %collective-permute-start.7) | collective-permute-done | bytes 368672 | tf_op jit(solution)/shard_map/ppermute | solution.py:32
  55.9 1.0 pack.2.mine
  57.0 1.3 collective-permute-start.10
  59.1 1.4 collective-permute-start.12
  61.0 1.3 copy-done.11
  62.2 13.0 %forward.1 = (bf16[320,1024]{1,0:T(8,128)(2,1)}, bf16[320,1024]{1,0:T(8,128)(2,1)}, bf16[320,1024]{1,0:T(8,128)(2,1)}, bf16[320,1024]{1,0:T(8,128)(2,1)}, bf16[3...) custom-call(bf16[320,3072]{1,0:T(8,128)(2,1)} %copy-done.1, bf16[320,3072]{1,0:T(8,128)(2,1)} %copy-done.11, ...), custom_call_target="tpu_custom_call" | custom-call | flops 8053063680 | tf_op jit(solution)/shard_map/forward/pallas_call | solution.py:289
  75.3 1.6 collective-permute-done.12.refs_3_
  76.9 2.3 %pack.3.grad.g_mine = bf16[320,3072]{1,0:T(8,128)(2,1)} custom-call(s32[4]{0:T(128)S(1)} %broadcast_multiply_fusion.starts, bf16[4,320,128]{2,1,0:T(8,128)(2,1)S(1)} %get-tuple-element.54.select, f32[4,320,128]{2,1,0:T(8,128)S(1)} %get-tuple-element.55.route_rows, bf16[128,3072]{1,0:T(8,128)(2,1)S(1)} %copy-done.14, ...), custom_call_target="tpu_custom_call" | custom-call | tf_op jit(solution)/shard_map/pack/pallas_call | solution.py:267
  79.2 2.8 %copy-done = bf16[1,1024,3072]{2,1,0:T(8,128)(2,1)S(1)} copy-done((bf16[1,1024,3072]{2,1,0:T(8,128)(2,1)S(1)}, bf16[1,1024,3072]{2,1,0:T(8,128)(2,1)}, u32[]{:S(2)}) %copy-start) | copy-done | bytes 6291480
  82.0 1.1 copy-done.20
  83.1 4.5 %backward.2 = (bf16[640,1024]{1,0:T(8,128)(2,1)S(1)}, bf16[640,1024]{1,0:T(8,128)(2,1)S(1)}) custom-call(bf16[320,3072]{1,0:T(8,128)(2,1)} %pack.3.grad.g_mine, bf16[1,1024,3072]{2,1,0:T(8,128)(2,1)S(1)} %copy-done, bf16[320,1024]{1,0:T(8,128)(2,1)S(1)} %copy-done.19, bf16[320,1024]{1,0:T(8,128)(2,1)S(1)} %copy-done.20), custom_call_target="tpu_custom_call" | custom-call | tf_op jit(solution)/shard_map/backward/pallas_call | solution.py:308
  87.6 4.6 %backward.3 = (bf16[640,1024]{1,0:T(8,128)(2,1)S(1)}, bf16[640,1024]{1,0:T(8,128)(2,1)S(1)}) custom-call(bf16[320,3072]{1,0:T(8,128)(2,1)} %collective-permute-done.13.grad.g_other, bf16[1,1024,3072]{2,1,0:T(8,128)(2,1)S(1)} %bitcast.26, bf16[320,1024]{1,0:T(8,128)(2,1)S(1)} %copy-done.17, ...), custom_call_target="tpu_custom_call", output_to_operand_aliasing={{0}: (4, {}), {1}: (5, {})} | custom-call | tf_op jit(solution)/shard_map/backward/pallas_call | solution.py:308
  92.2 2.2 %fusion.3 = f32[640,1536]{1,0:T(8,128)S(1)} fusion(bf16[640,1024]{1,0:T(8,128)(2,1)S(1)} %get-tuple-element.75.d_up, bf16[1,3072,1024]{2,1,0:T(8,128)(2,1)S(1)} %bitcast.28), kind=kOutput, calls=%fused_computation.5 | convolution fusion | flops 2013265920 | bytes 8388608 | tf_op jit(solution)/shard_map/dot_general | solution.py:20
  94.8 2.2 %add_convert_fusion.1.part = bf16[640,1536]{1,0:T(8,128)(2,1)S(1)} fusion(f32[640,1536]{1,0:T(8,128)S(1)} %fusion.3, bf16[640,1024]{1,0:T(8,128)(2,1)S(1)} %get-tuple-element.74.d_gate, bf16[1,3072,1024]{2,1,0:T(8,128)(2,1)S(1)} %bitcast.30), kind=kOutput, calls=%fused_computation.1 | convolution fusion | flops 2015232000 | bytes 10354688 | tf_op jit(solution)/shard_map/dot_general | solution.py:20
  97.6 2.2 %fusion = f32[640,1536]{1,0:T(8,128)S(1)} fusion(bf16[640,1024]{1,0:T(8,128)(2,1)S(1)} %get-tuple-element.75.d_up, bf16[1,3072,1024]{2,1,0:T(8,128)(2,1)S(1)} %bitcast.28), kind=kOutput, calls=%fused_computation.2 | convolution fusion | flops 2013265920 | bytes 8388608 | tf_op jit(solution)/shard_map/dot_general | solution.py:20
  99.9 2.2 %add_convert_fusion.part = bf16[640,1536]{1,0:T(8,128)(2,1)S(1)} fusion(f32[640,1536]{1,0:T(8,128)S(1)} %fusion, bf16[640,1024]{1,0:T(8,128)(2,1)S(1)} %get-tuple-element.74.d_gate, bf16[1,3072,1024]{2,1,0:T(8,128)(2,1)S(1)} %bitcast.30), kind=kOutput, calls=%fused_computation | convolution fusion | flops 2015232000 | bytes 10354688 | tf_op jit(solution)/shard_map/dot_general | solution.py:20
  102.3 1.4 merge.2
  104.5 1.5 collective-permute-start.16
  106.0 1.3 collective-permute-start.17
  107.2 1.5 merge.3
  109.5 1.5 collective-permute-start.26
  111.0 1.5 collective-permute-done.15.refs_1_
  113.2 1.7 %collective-permute-start.27 = (bf16[320,384]{1,0:T(8,128)(2,1)}, bf16[320,384]{1,0:T(8,128)(2,1)S(1)}, u32[]{:S(2)}, u32[]{:S(2)}) collective-permute-start(bf16[320,384]{1,0:T(8,128)(2,1)} %get-tuple-element.97), channel_id=1, source_target_pairs={{0,24},{8,16},{16,8},{24,0},{1,25},{9,17},{17,9},{25,1},{2,26},{10... | collective-permute-start | bytes 737288 | tf_op jit(solution)/shard_map/ppermute | solution.py:32
  114.9 1.5 all-gather.2.cloned.1.call-done.projection
  116.4 1.9 %copy-done.7 = bf16[512,3072]{1,0:T(8,128)(2,1)S(1)} copy-done((bf16[512,3072]{1,0:T(8,128)(2,1)S(1)}, bf16[512,3072]{1,0:T(8,128)(2,1)}, u32[]{:S(2)}) %copy-start.7) | copy-done | bytes 3145752
  118.3 1.5 copy-done.12
  119.9 6.9 %low.1 = (bf16[320,512]{1,0:T(8,128)(2,1)S(1)}, bf16[320,512]{1,0:T(8,128)(2,1)S(1)}, bf16[320,512]{1,0:T(8,128)(2,1)S(1)}, bf16[320,512]{1,0:T(8,128)(2,1)S(1)}) custom-call(bf16[320,3072]{1,0:T(8,128)(2,1)S(1)} %copy-done.2, bf16[320,3072]{1,0:T(8,128)(2,1)S(1)} %copy-done.12, bf16[320,3072]{1,0:T(8,128)(2,1)} %pack.3.grad.g_mine, ...), custom_call_target="tpu_custom_call" | custom-call | tf_op jit(solution)/shard_map/low/pallas_call | solution.py:363
  126.8 1.5 to_tokens.2
  130.1 2.7 %collective-permute-start.20 = (bf16[128,384]{1,0:T(8,128)(2,1)S(1)}, bf16[128,384]{1,0:T(8,128)(2,1)S(1)}, u32[]{:S(2)}, u32[]{:S(2)}) collective-permute-start(bf16[128,384]{1,0:T(8,128)(2,1)S(1)} %get-tuple-element.89), channel_id=1, source_target_pairs={{0,6},{1,7},{2,4},{3,5},{4,2},{5,3},{6,0},{7,1},{8,14},{9,15},{10,... | collective-permute-start | bytes 294920 | tf_op jit(solution)/shard_map/ppermute | solution.py:44
  132.8 6.0 %momentum.1 = (f32[1,512,1024]{2,1,0:T(8,128)}, f32[1,512,1024]{2,1,0:T(8,128)}, f32[1,1024,512]{2,1,0:T(8,128)}) custom-call(bf16[320,512]{1,0:T(8,128)(2,1)S(1)} %get-tuple-element.78.lt0, bf16[320,512]{1,0:T(8,128)(2,1)S(1)} %get-tuple-element.79.lt1, bf16[320,512]{1,0:T(8,128)(2,1)S(1)} %get-tuple-element.80.lg0, ...), custom_call_target="tpu_custom_call" | custom-call | tf_op jit(solution)/shard_map/momentum/pallas_call | solution.py:376
  139.5 1.7 %collective-permute-start.29 = (bf16[128,384]{1,0:T(8,128)(2,1)S(1)}, bf16[128,384]{1,0:T(8,128)(2,1)S(1)}, u32[]{:S(2)}, u32[]{:S(2)}) collective-permute-start(bf16[128,384]{1,0:T(8,128)(2,1)S(1)} %get-tuple-element.100), channel_id=1, source_target_pairs={{0,4},{1,5},{2,6},{3,7},{4,0},{5,1},{6,2},{7,3},{8,12},{9,13},{10,... | collective-permute-start | bytes 294920 | tf_op jit(solution)/shard_map/ppermute | solution.py:44
  141.2 2.7 %collective-permute-start.30 = (bf16[128,384]{1,0:T(8,128)(2,1)S(1)}, bf16[128,384]{1,0:T(8,128)(2,1)S(1)}, u32[]{:S(2)}, u32[]{:S(2)}) collective-permute-start(bf16[128,384]{1,0:T(8,128)(2,1)S(1)} %get-tuple-element.101), channel_id=1, source_target_pairs={{0,6},{1,7},{2,4},{3,5},{4,2},{5,3},{6,0},{7,1},{8,14},{9,15},{10,... | collective-permute-start | bytes 294920 | tf_op jit(solution)/shard_map/ppermute | solution.py:44
  143.9 2.3 %collective-permute-start.23 = (bf16[128,384]{1,0:T(8,128)(2,1)S(1)}, bf16[128,384]{1,0:T(8,128)(2,1)S(1)}, u32[]{:S(2)}, u32[]{:S(2)}) collective-permute-start(bf16[128,384]{1,0:T(8,128)(2,1)S(1)} %add_convert_fusion.3.refs_0_), channel_id=1, source_target_pairs={{0,24},{8,16},{16,8},{24,0},{1,25},{9,17},{17,9},{25,1},{2,26},{10... | collective-permute-start | bytes 294920 | tf_op jit(solution)/shard_map/ppermute | solution.py:32
  147.5 2.3 %collective-permute-done.29 = bf16[128,384]{1,0:T(8,128)(2,1)S(1)} collective-permute-done((bf16[128,384]{1,0:T(8,128)(2,1)S(1)}, bf16[128,384]{1,0:T(8,128)(2,1)S(1)}, u32[]{:S(2)}, u32[]{:S(2)}) %collective-permute-start.29) | collective-permute-done | bytes 98336 | tf_op jit(solution)/shard_map/ppermute | solution.py:44
  149.9 2.3 %collective-permute-start.33 = (bf16[128,384]{1,0:T(8,128)(2,1)S(1)}, bf16[128,384]{1,0:T(8,128)(2,1)S(1)}, u32[]{:S(2)}, u32[]{:S(2)}) collective-permute-start(bf16[128,384]{1,0:T(8,128)(2,1)S(1)} %add_convert_fusion.2.refs_4_), channel_id=1, source_target_pairs={{0,24},{8,16},{16,8},{24,0},{1,25},{9,17},{17,9},{25,1},{2,26},{10... | collective-permute-start | bytes 294920 | tf_op jit(solution)/shard_map/ppermute | solution.py:32
  153.4 2.0 %collective-permute-done.33.refs_7_ = bf16[128,384]{1,0:T(8,128)(2,1)S(1)} collective-permute-done((bf16[128,384]{1,0:T(8,128)(2,1)S(1)}, bf16[128,384]{1,0:T(8,128)(2,1)S(1)}, u32[]{:S(2)}, u32[]{:S(2)}) %collective-permute-start.33) | collective-permute-done | bytes 98336 | tf_op jit(solution)/shard_map/ppermute | solution.py:32
  155.4 1.4 collective-permute-done.32.refs_6_
  157.3 1.5 place.1
  (119 shorter events, 15.3 us)
Async XLA Ops:
  7.2 48.8 %copy-start.13 = (bf16[128,3072]{1,0:T(8,128)(2,1)S(1)}, bf16[128,3072]{1,0:T(8,128)(2,1)}, u32[]{:S(2)}) copy-start(bf16[128,3072]{1,0:T(8,128)(2,1)} %whole.2) | copy-start | bytes 2359300
  7.2 109.2 %all-gather.2.cloned.1.call-start = ((), (), s32[]{:S(2)}) async-start(), calls=%async_computation | async-start | bytes 3538944 | tf_op jit(solution)/shard_map/all_gather | solution.py:360
  9.6 11.5 %collective-permute-start.2 = (bf16[144,768]{1,0:T(8,128)(2,1)S(1)}, bf16[144,768]{1,0:T(8,128)(2,1)S(1)}, u32[]{:S(2)}, u32[]{:S(2)}) collective-permute-start(bf16[144,768]{1,0:T(8,128)(2,1)S(1)} %fusion.11), channel_id=1, source_target_pairs={{0,6},{1,7},{2,4},{3,5},{4,2},{5,3},{6,0},{7,1},{8,14},{9,15},{10,... | collective-permute-start | bytes 663560 | tf_op jit(solution)/shard_map/ppermute | solution.py:44
  14.8 18.8 %collective-permute-start.1 = (bf16[144,768]{1,0:T(8,128)(2,1)S(1)}, bf16[144,768]{1,0:T(8,128)(2,1)S(1)}, u32[]{:S(2)}, u32[]{:S(2)}) collective-permute-start(bf16[144,768]{1,0:T(8,128)(2,1)S(1)} %fusion.11), channel_id=1, source_target_pairs={{0,4},{1,5},{2,6},{3,7},{4,0},{5,1},{6,2},{7,3},{8,12},{9,13},{10,... | collective-permute-start | bytes 663560 | tf_op jit(solution)/shard_map/ppermute | solution.py:44
  14.8 18.8 %collective-permute-start = (bf16[144,768]{1,0:T(8,128)(2,1)S(1)}, bf16[144,768]{1,0:T(8,128)(2,1)S(1)}, u32[]{:S(2)}, u32[]{:S(2)}) collective-permute-start(bf16[144,768]{1,0:T(8,128)(2,1)S(1)} %fusion.11), channel_id=1, source_target_pairs={{0,2},{1,3},{2,0},{3,1},{4,6},{5,7},{6,4},{7,5},{8,10},{9,11},{10,... | collective-permute-start | bytes 663560 | tf_op jit(solution)/shard_map/ppermute | solution.py:44
  33.6 7.9 %collective-permute-start.5 = (bf16[128,768]{1,0:T(8,128)(2,1)S(1)}, bf16[128,768]{1,0:T(8,128)(2,1)S(1)}, u32[]{:S(2)}, u32[]{:S(2)}) collective-permute-start(bf16[128,768]{1,0:T(8,128)(2,1)S(1)} %constant_dynamic-slice_fusion), channel_id=1, source_target_pairs={{0,6},{1,7},{2,4},{3,5},{4,2},{5,3},{6,0},{7,1},{8,14},{9,15},{10,... | collective-permute-start | bytes 589832 | tf_op jit(solution)/shard_map/ppermute | solution.py:44
  37.8 16.1 %collective-permute-start.6 = (bf16[240,768]{1,0:T(8,128)(2,1)S(1)}, bf16[240,768]{1,0:T(8,128)(2,1)S(1)}, u32[]{:S(2)}, u32[]{:S(2)}) collective-permute-start(bf16[240,768]{1,0:T(8,128)(2,1)S(1)} %get-tuple-element.60), channel_id=1, source_target_pairs={{0,8},{8,0},{16,24},{24,16},{1,9},{9,1},{17,25},{25,17},{2,10},{10... | collective-permute-start | bytes 1105928 | tf_op jit(solution)/shard_map/ppermute | solution.py:32
  39.3 16.6 %collective-permute-start.7 = (bf16[240,768]{1,0:T(8,128)(2,1)S(1)}, bf16[240,768]{1,0:T(8,128)(2,1)S(1)}, u32[]{:S(2)}, u32[]{:S(2)}) collective-permute-start(bf16[240,768]{1,0:T(8,128)(2,1)S(1)} %get-tuple-element.61), channel_id=1, source_target_pairs={{0,16},{8,24},{16,0},{24,8},{1,17},{9,25},{17,1},{25,9},{2,18},{10... | collective-permute-start | bytes 1105928 | tf_op jit(solution)/shard_map/ppermute | solution.py:32
  40.9 15.1 %collective-permute-start.8 = (bf16[240,768]{1,0:T(8,128)(2,1)S(1)}, bf16[240,768]{1,0:T(8,128)(2,1)S(1)}, u32[]{:S(2)}, u32[]{:S(2)}) collective-permute-start(bf16[240,768]{1,0:T(8,128)(2,1)S(1)} %get-tuple-element.62), channel_id=1, source_target_pairs={{0,24},{8,16},{16,8},{24,0},{1,25},{9,17},{17,9},{25,1},{2,26},{10... | collective-permute-start | bytes 1105928 | tf_op jit(solution)/shard_map/ppermute | solution.py:32
  41.3 9.9 %collective-permute-start.4 = (bf16[128,768]{1,0:T(8,128)(2,1)S(1)}, bf16[128,768]{1,0:T(8,128)(2,1)S(1)}, u32[]{:S(2)}, u32[]{:S(2)}) collective-permute-start(bf16[128,768]{1,0:T(8,128)(2,1)S(1)} %constant_dynamic-slice_fusion), channel_id=1, source_target_pairs={{0,4},{1,5},{2,6},{3,7},{4,0},{5,1},{6,2},{7,3},{8,12},{9,13},{10,... | collective-permute-start | bytes 589832 | tf_op jit(solution)/shard_map/ppermute | solution.py:44
  41.4 11.9 %collective-permute-start.3 = (bf16[128,768]{1,0:T(8,128)(2,1)S(1)}, bf16[128,768]{1,0:T(8,128)(2,1)S(1)}, u32[]{:S(2)}, u32[]{:S(2)}) collective-permute-start(bf16[128,768]{1,0:T(8,128)(2,1)S(1)} %constant_dynamic-slice_fusion), channel_id=1, source_target_pairs={{0,2},{1,3},{2,0},{3,1},{4,6},{5,7},{6,4},{7,5},{8,10},{9,11},{10,... | collective-permute-start | bytes 589832 | tf_op jit(solution)/shard_map/ppermute | solution.py:44
  56.9 4.0 %collective-permute-start.9 = (bf16[320,3072]{1,0:T(8,128)(2,1)S(1)}, bf16[320,3072]{1,0:T(8,128)(2,1)S(1)}, u32[]{:S(2)}, u32[]{:S(2)}) collective-permute-start(bf16[320,3072]{1,0:T(8,128)(2,1)S(1)} %pack.2.mine), channel_id=1, source_target_pairs={{0,1},{1,0},{2,3},{3,2},{4,5},{5,4},{6,7},{7,6},{8,9},{9,8},{10,11... | collective-permute-start | bytes 5898248 | tf_op jit(solution)/shard_map/ppermute | solution.py:36
  57.0 18.3 %collective-permute-start.10 = (bf16[240,768]{1,0:T(8,128)(2,1)S(1)}, bf16[240,768]{1,0:T(8,128)(2,1)S(1)}, u32[]{:S(2)}, u32[]{:S(2)}) collective-permute-start(bf16[240,768]{1,0:T(8,128)(2,1)S(1)} %get-tuple-element.65), channel_id=1, source_target_pairs={{0,8},{8,0},{16,24},{24,16},{1,9},{9,1},{17,25},{25,17},{2,10},{10... | collective-permute-start | bytes 1105928 | tf_op jit(solution)/shard_map/ppermute | solution.py:32
  58.3 17.0 %collective-permute-start.11 = (bf16[240,768]{1,0:T(8,128)(2,1)S(1)}, bf16[240,768]{1,0:T(8,128)(2,1)S(1)}, u32[]{:S(2)}, u32[]{:S(2)}) collective-permute-start(bf16[240,768]{1,0:T(8,128)(2,1)S(1)} %get-tuple-element.66), channel_id=1, source_target_pairs={{0,16},{8,24},{16,0},{24,8},{1,17},{9,25},{17,1},{25,9},{2,18},{10... | collective-permute-start | bytes 1105928 | tf_op jit(solution)/shard_map/ppermute | solution.py:32
  59.1 17.7 %copy-start.14 = (bf16[128,3072]{1,0:T(8,128)(2,1)S(1)}, bf16[128,3072]{1,0:T(8,128)(2,1)}, u32[]{:S(2)}) copy-start(bf16[128,3072]{1,0:T(8,128)(2,1)} %whole.3) | copy-start | bytes 2359300
  59.1 17.7 %collective-permute-start.12 = (bf16[240,768]{1,0:T(8,128)(2,1)S(1)}, bf16[240,768]{1,0:T(8,128)(2,1)S(1)}, u32[]{:S(2)}, u32[]{:S(2)}) collective-permute-start(bf16[240,768]{1,0:T(8,128)(2,1)S(1)} %get-tuple-element.67), channel_id=1, source_target_pairs={{0,24},{8,16},{16,8},{24,0},{1,25},{9,17},{17,9},{25,1},{2,26},{10... | collective-permute-start | bytes 1105928 | tf_op jit(solution)/shard_map/ppermute | solution.py:32
  76.9 10.7 %slice-start = ((s8[6291456]{0:T(1024)(128)(4,1)}), s8[2097152]{0:T(1024)(128)(4,1)S(1)}, s32[]{:S(2)}) async-start(s8[6291456]{0:T(1024)(128)(4,1)} %bitcast.25), calls=%async_computation.1 | async-start | bytes 4194304
  79.2 8.4 %collective-permute-start.13 = (bf16[320,3072]{1,0:T(8,128)(2,1)}, bf16[320,3072]{1,0:T(8,128)(2,1)}, u32[]{:S(2)}, u32[]{:S(2)}) collective-permute-start(bf16[320,3072]{1,0:T(8,128)(2,1)} %pack.3.grad.g_mine), channel_id=1, source_target_pairs={{0,1},{1,0},{2,3},{3,2},{4,5},{5,4},{6,7},{7,6},{8,9},{9,8},{10,11... | collective-permute-start | bytes 5898248 | tf_op jit(solution)/shard_map/ppermute | solution.py:36
  83.1 9.1 %slice-start.2 = ((s8[6291456]{0:T(1024)(128)(4,1)}), s8[4194304]{0:T(1024)(128)(4,1)S(1)}, s32[]{:S(2)}) async-start(s8[6291456]{0:T(1024)(128)(4,1)} %bitcast.27), calls=%async_computation.3 | async-start | bytes 8388608
  97.1 5.2 %collective-permute-start.14 = (bf16[320,1536]{1,0:T(8,128)(2,1)S(1)}, bf16[320,1536]{1,0:T(8,128)(2,1)S(1)}, u32[]{:S(2)}, u32[]{:S(2)}) collective-permute-start(bf16[320,1536]{1,0:T(8,128)(2,1)S(1)} %slice.24), channel_id=1, source_target_pairs={{0,1},{1,0},{2,3},{3,2},{4,5},{5,4},{6,7},{7,6},{8,9},{9,8},{10,11... | collective-permute-start | bytes 2949128 | tf_op jit(solution)/shard_map/ppermute | solution.py:36
  102.2 14.2 %copy-start.2 = (bf16[320,3072]{1,0:T(8,128)(2,1)S(1)}, bf16[320,3072]{1,0:T(8,128)(2,1)}, u32[]{:S(2)}) copy-start(bf16[320,3072]{1,0:T(8,128)(2,1)} %copy-done.1) | copy-start | bytes 5898244
  102.2 5.0 %collective-permute-start.24 = (bf16[320,1536]{1,0:T(8,128)(2,1)S(1)}, bf16[320,1536]{1,0:T(8,128)(2,1)S(1)}, u32[]{:S(2)}, u32[]{:S(2)}) collective-permute-start(bf16[320,1536]{1,0:T(8,128)(2,1)S(1)} %slice.25), channel_id=1, source_target_pairs={{0,1},{1,0},{2,3},{3,2},{4,5},{5,4},{6,7},{7,6},{8,9},{9,8},{10,11... | collective-permute-start | bytes 2949128 | tf_op jit(solution)/shard_map/ppermute | solution.py:36
  103.7 8.8 %copy-start.21 = (bf16[320,384]{1,0:T(8,128)(2,1)}, bf16[320,384]{1,0:T(8,128)(2,1)S(1)}, u32[]{:S(2)}) copy-start(bf16[320,384]{1,0:T(8,128)(2,1)S(1)} %get-tuple-element.82.refs_0_) | copy-start | bytes 737284
  103.7 8.8 %collective-permute-start.15 = (bf16[320,384]{1,0:T(8,128)(2,1)S(1)}, bf16[320,384]{1,0:T(8,128)(2,1)S(1)}, u32[]{:S(2)}, u32[]{:S(2)}) collective-permute-start(bf16[320,384]{1,0:T(8,128)(2,1)S(1)} %get-tuple-element.83), channel_id=1, source_target_pairs={{0,8},{8,0},{16,24},{24,16},{1,9},{9,1},{17,25},{25,17},{2,10},{10... | collective-permute-start | bytes 737288 | tf_op jit(solution)/shard_map/ppermute | solution.py:32
  104.5 22.3 %collective-permute-start.16 = (bf16[320,384]{1,0:T(8,128)(2,1)}, bf16[320,384]{1,0:T(8,128)(2,1)}, u32[]{:S(2)}, u32[]{:S(2)}) collective-permute-start(bf16[320,384]{1,0:T(8,128)(2,1)} %get-tuple-element.84), channel_id=1, source_target_pairs={{0,16},{8,24},{16,0},{24,8},{1,17},{9,25},{17,1},{25,9},{2,18},{10... | collective-permute-start | bytes 737288 | tf_op jit(solution)/shard_map/ppermute | solution.py:32
  106.0 20.8 %collective-permute-start.17 = (bf16[320,384]{1,0:T(8,128)(2,1)}, bf16[320,384]{1,0:T(8,128)(2,1)}, u32[]{:S(2)}, u32[]{:S(2)}) collective-permute-start(bf16[320,384]{1,0:T(8,128)(2,1)} %get-tuple-element.85), channel_id=1, source_target_pairs={{0,24},{8,16},{16,8},{24,0},{1,25},{9,17},{17,9},{25,1},{2,26},{10... | collective-permute-start | bytes 737288 | tf_op jit(solution)/shard_map/ppermute | solution.py:32
  108.8 21.3 %collective-permute-start.25 = (bf16[320,384]{1,0:T(8,128)(2,1)}, bf16[320,384]{1,0:T(8,128)(2,1)S(1)}, u32[]{:S(2)}, u32[]{:S(2)}) collective-permute-start(bf16[320,384]{1,0:T(8,128)(2,1)} %get-tuple-element.95), channel_id=1, source_target_pairs={{0,8},{8,0},{16,24},{24,16},{1,9},{9,1},{17,25},{25,17},{2,10},{10... | collective-permute-start | bytes 737288 | tf_op jit(solution)/shard_map/ppermute | solution.py:32
  109.5 29.4 %collective-permute-start.26 = (bf16[320,384]{1,0:T(8,128)(2,1)}, bf16[320,384]{1,0:T(8,128)(2,1)S(1)}, u32[]{:S(2)}, u32[]{:S(2)}) collective-permute-start(bf16[320,384]{1,0:T(8,128)(2,1)} %get-tuple-element.96), channel_id=1, source_target_pairs={{0,16},{8,24},{16,0},{24,8},{1,17},{9,25},{17,1},{25,9},{2,18},{10... | collective-permute-start | bytes 737288 | tf_op jit(solution)/shard_map/ppermute | solution.py:32
  113.2 25.7 %collective-permute-start.27 = (bf16[320,384]{1,0:T(8,128)(2,1)}, bf16[320,384]{1,0:T(8,128)(2,1)S(1)}, u32[]{:S(2)}, u32[]{:S(2)}) collective-permute-start(bf16[320,384]{1,0:T(8,128)(2,1)} %get-tuple-element.97), channel_id=1, source_target_pairs={{0,24},{8,16},{16,8},{24,0},{1,25},{9,17},{17,9},{25,1},{2,26},{10... | collective-permute-start | bytes 737288 | tf_op jit(solution)/shard_map/ppermute | solution.py:32
  119.8 13.0 %copy-start.4 = (bf16[640,1024]{1,0:T(8,128)(2,1)S(1)}, bf16[640,1024]{1,0:T(8,128)(2,1)}, u32[]{:S(2)}) copy-start(bf16[640,1024]{1,0:T(8,128)(2,1)} %copy-done.3) | copy-start | bytes 3932164
  119.8 13.0 %copy-start.6 = (bf16[640,1024]{1,0:T(8,128)(2,1)S(1)}, bf16[640,1024]{1,0:T(8,128)(2,1)}, u32[]{:S(2)}) copy-start(bf16[640,1024]{1,0:T(8,128)(2,1)} %copy-done.5) | copy-start | bytes 3932164
  119.8 13.0 %copy-start.8 = (f32[1,512,1024]{2,1,0:T(8,128)S(1)}, f32[1,512,1024]{2,1,0:T(8,128)}, u32[]{:S(2)}) copy-start(f32[1,512,1024]{2,1,0:T(8,128)} %mg.1) | copy-start | bytes 6291460
  119.8 13.0 %copy-start.9 = (f32[1,512,1024]{2,1,0:T(8,128)S(1)}, f32[1,512,1024]{2,1,0:T(8,128)}, u32[]{:S(2)}) copy-start(f32[1,512,1024]{2,1,0:T(8,128)} %mu.1) | copy-start | bytes 6291460
  119.8 13.0 %copy-start.10 = (f32[1,1024,512]{2,1,0:T(8,128)S(1)}, f32[1,1024,512]{2,1,0:T(8,128)}, u32[]{:S(2)}) copy-start(f32[1,1024,512]{2,1,0:T(8,128)} %md.1) | copy-start | bytes 6291460
  119.8 13.0 %copy-start.15 = (bf16[320,1024]{1,0:T(8,128)(2,1)S(1)}, bf16[320,1024]{1,0:T(8,128)(2,1)}, u32[]{:S(2)}) copy-start(bf16[320,1024]{1,0:T(8,128)(2,1)} %get-tuple-element.63.h0) | copy-start | bytes 1966084
  119.9 13.0 %copy-start.16 = (bf16[320,1024]{1,0:T(8,128)(2,1)S(1)}, bf16[320,1024]{1,0:T(8,128)(2,1)}, u32[]{:S(2)}) copy-start(bf16[320,1024]{1,0:T(8,128)(2,1)} %get-tuple-element.92.h1) | copy-start | bytes 1966084
  128.3 12.8 %collective-permute-start.18 = (bf16[128,384]{1,0:T(8,128)(2,1)S(1)}, bf16[128,384]{1,0:T(8,128)(2,1)S(1)}, u32[]{:S(2)}, u32[]{:S(2)}) collective-permute-start(bf16[128,384]{1,0:T(8,128)(2,1)S(1)} %get-tuple-element.87), channel_id=1, source_target_pairs={{0,2},{1,3},{2,0},{3,1},{4,6},{5,7},{6,4},{7,5},{8,10},{9,11},{10,... | collective-permute-start | bytes 294920 | tf_op jit(solution)/shard_map/ppermute | solution.py:44
  129.2 14.7 %collective-permute-start.19 = (bf16[128,384]{1,0:T(8,128)(2,1)S(1)}, bf16[128,384]{1,0:T(8,128)(2,1)S(1)}, u32[]{:S(2)}, u32[]{:S(2)}) collective-permute-start(bf16[128,384]{1,0:T(8,128)(2,1)S(1)} %get-tuple-element.88), channel_id=1, source_target_pairs={{0,4},{1,5},{2,6},{3,7},{4,0},{5,1},{6,2},{7,3},{8,12},{9,13},{10,... | collective-permute-start | bytes 294920 | tf_op jit(solution)/shard_map/ppermute | solution.py:44
  130.1 13.7 %collective-permute-start.20 = (bf16[128,384]{1,0:T(8,128)(2,1)S(1)}, bf16[128,384]{1,0:T(8,128)(2,1)S(1)}, u32[]{:S(2)}, u32[]{:S(2)}) collective-permute-start(bf16[128,384]{1,0:T(8,128)(2,1)S(1)} %get-tuple-element.89), channel_id=1, source_target_pairs={{0,6},{1,7},{2,4},{3,5},{4,2},{5,3},{6,0},{7,1},{8,14},{9,15},{10,... | collective-permute-start | bytes 294920 | tf_op jit(solution)/shard_map/ppermute | solution.py:44
  139.4 7.4 %collective-permute-start.28 = (bf16[128,384]{1,0:T(8,128)(2,1)S(1)}, bf16[128,384]{1,0:T(8,128)(2,1)S(1)}, u32[]{:S(2)}, u32[]{:S(2)}) collective-permute-start(bf16[128,384]{1,0:T(8,128)(2,1)S(1)} %get-tuple-element.99), channel_id=1, source_target_pairs={{0,2},{1,3},{2,0},{3,1},{4,6},{5,7},{6,4},{7,5},{8,10},{9,11},{10,... | collective-permute-start | bytes 294920 | tf_op jit(solution)/shard_map/ppermute | solution.py:44
  139.5 10.3 %collective-permute-start.29 = (bf16[128,384]{1,0:T(8,128)(2,1)S(1)}, bf16[128,384]{1,0:T(8,128)(2,1)S(1)}, u32[]{:S(2)}, u32[]{:S(2)}) collective-permute-start(bf16[128,384]{1,0:T(8,128)(2,1)S(1)} %get-tuple-element.100), channel_id=1, source_target_pairs={{0,4},{1,5},{2,6},{3,7},{4,0},{5,1},{6,2},{7,3},{8,12},{9,13},{10,... | collective-permute-start | bytes 294920 | tf_op jit(solution)/shard_map/ppermute | solution.py:44
  141.2 8.6 %collective-permute-start.30 = (bf16[128,384]{1,0:T(8,128)(2,1)S(1)}, bf16[128,384]{1,0:T(8,128)(2,1)S(1)}, u32[]{:S(2)}, u32[]{:S(2)}) collective-permute-start(bf16[128,384]{1,0:T(8,128)(2,1)S(1)} %get-tuple-element.101), channel_id=1, source_target_pairs={{0,6},{1,7},{2,4},{3,5},{4,2},{5,3},{6,0},{7,1},{8,14},{9,15},{10,... | collective-permute-start | bytes 294920 | tf_op jit(solution)/shard_map/ppermute | solution.py:44
  143.9 8.8 %collective-permute-start.23 = (bf16[128,384]{1,0:T(8,128)(2,1)S(1)}, bf16[128,384]{1,0:T(8,128)(2,1)S(1)}, u32[]{:S(2)}, u32[]{:S(2)}) collective-permute-start(bf16[128,384]{1,0:T(8,128)(2,1)S(1)} %add_convert_fusion.3.refs_0_), channel_id=1, source_target_pairs={{0,24},{8,16},{16,8},{24,0},{1,25},{9,17},{17,9},{25,1},{2,26},{10... | collective-permute-start | bytes 294920 | tf_op jit(solution)/shard_map/ppermute | solution.py:32
  146.2 7.2 %collective-permute-start.22 = (bf16[128,384]{1,0:T(8,128)(2,1)S(1)}, bf16[128,384]{1,0:T(8,128)(2,1)S(1)}, u32[]{:S(2)}, u32[]{:S(2)}) collective-permute-start(bf16[128,384]{1,0:T(8,128)(2,1)S(1)} %add_convert_fusion.3.refs_0_), channel_id=1, source_target_pairs={{0,16},{8,24},{16,0},{24,8},{1,17},{9,25},{17,1},{25,9},{2,18},{10... | collective-permute-start | bytes 294920 | tf_op jit(solution)/shard_map/ppermute | solution.py:32
  146.8 6.7 %collective-permute-start.21 = (bf16[128,384]{1,0:T(8,128)(2,1)S(1)}, bf16[128,384]{1,0:T(8,128)(2,1)S(1)}, u32[]{:S(2)}, u32[]{:S(2)}) collective-permute-start(bf16[128,384]{1,0:T(8,128)(2,1)S(1)} %add_convert_fusion.3.refs_0_), channel_id=1, source_target_pairs={{0,8},{8,0},{16,24},{24,16},{1,9},{9,1},{17,25},{25,17},{2,10},{10... | collective-permute-start | bytes 294920 | tf_op jit(solution)/shard_map/ppermute | solution.py:32
  149.9 5.6 %collective-permute-start.33 = (bf16[128,384]{1,0:T(8,128)(2,1)S(1)}, bf16[128,384]{1,0:T(8,128)(2,1)S(1)}, u32[]{:S(2)}, u32[]{:S(2)}) collective-permute-start(bf16[128,384]{1,0:T(8,128)(2,1)S(1)} %add_convert_fusion.2.refs_4_), channel_id=1, source_target_pairs={{0,24},{8,16},{16,8},{24,0},{1,25},{9,17},{17,9},{25,1},{2,26},{10... | collective-permute-start | bytes 294920 | tf_op jit(solution)/shard_map/ppermute | solution.py:32
  152.2 4.6 %collective-permute-start.32 = (bf16[128,384]{1,0:T(8,128)(2,1)S(1)}, bf16[128,384]{1,0:T(8,128)(2,1)S(1)}, u32[]{:S(2)}, u32[]{:S(2)}) collective-permute-start(bf16[128,384]{1,0:T(8,128)(2,1)S(1)} %add_convert_fusion.2.refs_4_), channel_id=1, source_target_pairs={{0,16},{8,24},{16,0},{24,8},{1,17},{9,25},{17,1},{25,9},{2,18},{10... | collective-permute-start | bytes 294920 | tf_op jit(solution)/shard_map/ppermute | solution.py:32
  152.7 4.6 %collective-permute-start.31 = (bf16[128,384]{1,0:T(8,128)(2,1)S(1)}, bf16[128,384]{1,0:T(8,128)(2,1)S(1)}, u32[]{:S(2)}, u32[]{:S(2)}) collective-permute-start(bf16[128,384]{1,0:T(8,128)(2,1)S(1)} %add_convert_fusion.2.refs_4_), channel_id=1, source_target_pairs={{0,8},{8,0},{16,24},{24,16},{1,9},{9,1},{17,25},{25,17},{2,10},{10... | collective-permute-start | bytes 294920 | tf_op jit(solution)/shard_map/ppermute | solution.py:32
  (18 other events, 71.9 us)
Sparse Core Ops, SparseCore 0:
  79.3 37.0 all-gather.1
